TPU v7x, 32 devices: a whole 2x2x4 slice. The times are simulated.
32 devices in a mesh: seq: 8 (over z, x), tensor: 4 (over y, core).
Axes of the slice: x: 2, y: 2, z: 4, core: 2. Of those that a mesh axis runs over, the one named last changes fastest.
Arguments:
- queries: bfloat16 [7168, 2048], P('seq', 'tensor'), may hold values from -256 to 256
- db_states: bfloat16 [128, 64, 896], P('seq', None, 'tensor'), may hold values from -4096 to 4096
- enc_gain: float32 [896], replicated, may hold values from 0.1 to 1.9
- kv_weight: bfloat16 [896, 2, 2048], P(None, None, 'tensor'), may hold values from -0.1875 to 0.1875
- shard_ids: int32 [112, 2], P('seq'), may hold values from 0 to 7, as said below
- offsets: int32 [112, 2], P('seq'), may hold values from 0 to 14
Outputs:
- attention_out: bfloat16 [7168, 2048], P('seq', 'tensor')
Inputs may be any that keep to these rules, and one draw needn't show every extreme that they name: `shard_ids`: the neighbours named by the 14 groups of one device lie at most 4 in any one shard, and some shard is named exactly 4 times by the groups of every device.
All inputs are finite; a program needn't handle non-finite values.
Results may differ from a plain program's by a relative error of at most 0.0087.
Values may be sent and summed in bfloat16 or wider, within the bound.
A program may use at most 64 MiB of HBM per device.

v0:
```python
import math

import jax
import jax.numpy as jnp
from jax import lax
from jax.sharding import PartitionSpec as P

HEAD_DIM = 128


epsilon = 1e-06


def passed_along(block, axis, distance):
    devices = range(lax.axis_size(axis))
    route = [(i - distance, i) for i in devices if i - distance in devices]
    return lax.ppermute(block, axis, route)


def attend(query_win, kv_win):
    scores = jnp.einsum(
        "wqhd,wkhd->whqk", query_win, kv_win[:, :, 0], preferred_element_type=jnp.float32
    ) / math.sqrt(HEAD_DIM)
    highest = jnp.max(scores, axis=-1, keepdims=True)
    expo = jnp.exp(scores - highest)
    weights = (expo / jnp.sum(expo, axis=-1, keepdims=True)).astype(jnp.bfloat16)
    mixed = jnp.einsum(
        "whqk,wkhd->wqhd", weights, kv_win[:, :, 1], preferred_element_type=jnp.float32
    ).astype(jnp.bfloat16)
    return mixed.reshape(query_win.shape[0] * query_win.shape[1], -1)


def per_device(queries, db_states, enc_gain, kv_weight, shard_ids, offsets):
    seq_count = lax.axis_size("seq")
    group_count = shard_ids.shape[0]
    neigh_count = 2 * group_count
    slot_cap = (neigh_count + seq_count - 1) // seq_count
    group_len = db_states.shape[1]
    enc_width = kv_weight.shape[0]
    head_count = kv_weight.shape[2] // HEAD_DIM
    tok_count = queries.shape[0]
    query_cols = queries.shape[1]
    projection = kv_weight.reshape(enc_width, -1)
    token_rows = neigh_count * 2 * group_len
    neigh_shard = shard_ids.reshape(neigh_count)
    neigh_offset = offsets.reshape(neigh_count)
    owners = jnp.arange(seq_count, dtype=jnp.int32)
    onehot = (neigh_shard[:, None] == owners[None, :]).astype(jnp.int32)
    before = jnp.cumsum(onehot, axis=0) - onehot
    order_rank = jnp.sum(before * onehot, axis=1)
    slot_index = neigh_shard * slot_cap + order_rank
    table = jnp.zeros((seq_count * slot_cap,), jnp.int32).at[slot_index].set(neigh_offset + 1)
    wanted = lax.all_to_all(
        table.reshape(seq_count, slot_cap), "seq", split_axis=0, concat_axis=0, tiled=True
    )
    first_group = jnp.maximum(wanted - 1, 0)
    stored = db_states.reshape(db_states.shape[0], -1)
    outgoing = jnp.stack(
        [jnp.take(stored, first_group, axis=0), jnp.take(stored, first_group + 1, axis=0)], axis=2
    )
    incoming = lax.all_to_all(outgoing, "seq", split_axis=0, concat_axis=0, tiled=True)
    picked = jnp.take(incoming.reshape(seq_count * slot_cap, 2, -1), slot_index, axis=0)
    enc_rows = picked.reshape(token_rows, -1)
    as_float = lax.all_gather(enc_rows, "tensor", axis=1, tiled=True).astype(jnp.float32)
    scaled = (as_float * enc_gain[None, :]).astype(jnp.bfloat16)
    kv_sum = jnp.dot(scaled, projection, preferred_element_type=jnp.float32)
    kv_sum, square_sum = (kv_sum, jnp.sum(as_float * as_float, axis=1))
    inv_rms = lax.rsqrt(square_sum / enc_width + epsilon)
    keys_values = (kv_sum * inv_rms[:, None]).astype(jnp.bfloat16)
    kv_groups = keys_values.reshape(group_count, 4 * group_len, 2, head_count, HEAD_DIM)
    previous = passed_along(kv_groups[group_count - 1], "seq", 1)
    padded = jnp.concatenate(
        [
            jnp.zeros((1, query_cols), jnp.bfloat16),
            queries,
            jnp.zeros((group_len - 1, query_cols), jnp.bfloat16),
        ],
        axis=0,
    )
    windows = padded.reshape(group_count + 1, group_len, head_count, HEAD_DIM)
    attended = attend(windows, jnp.concatenate([previous[None], kv_groups], axis=0))
    result = attended[1 : tok_count + 1]
    return result


def solution(mesh):
    return jax.shard_map(
        per_device,
        mesh=mesh,
        in_specs=(
            P("seq", "tensor"),
            P("seq", None, "tensor"),
            P(),
            P(None, None, "tensor"),
            P("seq", None),
            P("seq", None),
        ),
        out_specs=P("seq", "tensor"),
        check_vma=False,
    )
```

profile of v0, /device:TPU:24, one launch (start us, length us, event | category | flops | bytes accessed | tf_op | source)
XLA Modules:
  0.0 212.1 jit_solution(16390059754301208129)
XLA Ops:
  10.8 6.0 %all-to-all-start = ((s32[8,1,4]{2,1,0:T(1,128)}), s32[8,1,4]{2,1,0:T(1,128)S(1)}, u32[]{:S(2)}, u32[]{:S(2)}) async-start(s32[8,1,4]{2,1,0:T(1,128)} %bitcast.2), calls=%async_computation | async-start | bytes 8192 | tf_op jit(solution)/shard_map/all_to_all | solution.py:53
  16.8 1.9 reshape.89
  18.7 1.2 all-to-all-done
  24.4 2.5 %pad_maximum_fusion.1 = bf16[8,4,2,14336]{3,1,2,0:T(4,128)(2,1)} fusion(bf16[8,4,1,14336]{3,1,2,0:T(4,128)(2,1)S(1)} %get-tuple-element.10, bf16[8,4,1,14336]{3,1,2,0:T(4,128)(2,1)S(1)} %get-tuple-element.11), kind=kLoop, calls=%fused_computation.27 | loop fusion | flops 917504 | bytes 3670016 | tf_op jit(solution)/shard_map/stack | solution.py:58
  26.9 6.8 %all-to-all-start.1 = ((bf16[8,4,2,14336]{3,1,2,0:T(4,128)(2,1)}), bf16[8,4,2,14336]{3,1,2,0:T(4,128)(2,1)S(1)}, u32[]{:S(2)}, u32[]{:S(2)}) async-start(bf16[8,4,2,14336]{3,1,2,0:T(4,128)(2,1)} %pad_maximum_fusion.1), calls=%async_computation.1 | async-start | bytes 3670016 | tf_op jit(solution)/shard_map/all_to_all | solution.py:61
  33.7 38.8 %all-to-all-done.1 = bf16[8,4,2,14336]{3,1,2,0:T(4,128)(2,1)S(1)} async-done(((bf16[8,4,2,14336]{3,1,2,0:T(4,128)(2,1)}), bf16[8,4,2,14336]{3,1,2,0:T(4,128)(2,1)S(1)}, u32[]{:S(2)}, u32[]{:S(2)}) %all-to-all-start.1) | async-done | bytes 1835040 | tf_op jit(solution)/shard_map/all_to_all | solution.py:61
  72.5 3.1 %copy.56 = bf16[8,4,2,14336]{3,2,1,0:T(2,128)(2,1)} copy(bf16[8,4,2,14336]{3,1,2,0:T(4,128)(2,1)S(1)} %all-to-all-done.1) | data formatting | bytes 3670016 | tf_op jit(solution)/shard_map/all_to_all | solution.py:61
  75.6 5.3 %gather_fusion = bf16[28,2,14336]{2,1,0:T(2,128)(2,1)S(1)} fusion(bf16[32,2,14336]{2,1,0:T(2,128)(2,1)} %bitcast.48, s32[1024]{0:T(1024)S(1)} %pad_clamp_fusion), kind=kCustom, calls=%fused_computation.2 | custom fusion | bytes 3211376 | tf_op jit(solution)/shard_map/jit(_take)/gather | solution.py:62
  80.9 1.5 broadcast_select_fusion
  82.4 2.6 %select_n.35 = bf16[3584,224]{1,0:T(8,128)(2,1)S(1)} reshape(bf16[28,2,14336]{2,1,0:T(2,128)(2,1)S(1)} %broadcast_select_fusion) | data formatting | bytes 3211264 | tf_op jit(solution)/shard_map/jit(_take)/select_n | solution.py:62
  85.1 2.6 %copy.57 = bf16[3584,224]{0,1:T(8,128)(2,1)} copy(bf16[3584,224]{1,0:T(8,128)(2,1)S(1)} %select_n.35) | data formatting | bytes 3211264 | tf_op jit(solution)/shard_map/jit(_take)/select_n | solution.py:62
  87.7 2.0 copy.65
  89.7 46.5 %all-gather.2.cloned.1.call-done = bf16[3584,896]{0,1:T(8,128)(2,1)} async-done(((bf16[3584,224]{0,1:T(8,128)(2,1)}), bf16[3584,896]{0,1:T(8,128)(2,1)}) %all-gather.2.cloned.1.call-update) | async-done | bytes 6422544 | tf_op jit(solution)/shard_map/all_gather | solution.py:64
  136.1 4.3 %fusion.2 = f32[3584]{0:T(1024)S(1)} fusion(bf16[3584,896]{0,1:T(8,128)(2,1)} %all-gather.2.cloned.1.call-done), kind=kLoop, calls=%fused_computation.9 | loop fusion | flops 9630208 | bytes 6436864 | tf_op jit(solution)/shard_map/reduce_sum | solution.py:67
  140.8 8.7 %multiply_convert_fusion = bf16[3584,1024]{0,1:T(8,128)(2,1)S(1)} fusion(bf16[896,1024]{1,0:T(8,128)(2,1)S(1)} %bitcast.53, f32[3584]{0:T(1024)S(1)} %add_rsqrt_fusion, bf16[3584,896]{0,1:T(8,128)(2,1)S(1)} %copy-done.1, f32[896]{0:T(1024)S(1)} %copy-done.4), kind=kOutput, calls=%fused_computation.7 | convolution fusion | flops 6593642496 | bytes 15615488 | tf_op jit(solution)/shard_map/dot_general | solution.py:66
  149.5 3.0 %copy-done = bf16[3584,1024]{0,1:T(8,128)(2,1)} copy-done((bf16[3584,1024]{0,1:T(8,128)(2,1)}, bf16[3584,1024]{0,1:T(8,128)(2,1)S(1)}, u32[]{:S(2)}) %copy-start) | copy-done | bytes 7340056
  153.5 3.3 %collective-permute-start = (bf16[256,2,4,128]{3,0,2,1:T(8,128)(2,1)}, bf16[256,2,4,128]{3,0,2,1:T(8,128)(2,1)S(1)}, u32[]{:S(2)}, u32[]{:S(2)}) collective-permute-start(bf16[256,2,4,128]{3,0,2,1:T(8,128)(2,1)} %copy.58), channel_id=1, source_target_pairs={{0,4},{4,8},{8,12},{12,16},{16,20},{20,24},{24,28},{1,5},{5,9},{9,... | collective-permute-start | bytes 1572872 | tf_op jit(solution)/shard_map/ppermute | solution.py:17
  157.6 13.7 %reshape.139 = bf16[14,256,2,4,128]{1,0,4,3,2:T(8,128)(2,1)} reshape(bf16[3584,1024]{0,1:T(8,128)(2,1)} %copy-done) | data formatting | bytes 14680064 | tf_op jit(solution)/shard_map/reshape | solution.py:70
  171.3 14.2 %copy.60 = bf16[14,256,2,4,128]{4,1,3,0,2:T(8,128)(2,1)} copy(bf16[14,256,2,4,128]{1,0,4,3,2:T(8,128)(2,1)} %reshape.139) | data formatting | bytes 14680064 | tf_op jit(solution)/shard_map/reshape | solution.py:70
  185.5 3.1 %fusion.7 = f32[15,4,64,256]{3,2,1,0:T(8,128)S(1)} fusion(bf16[1,256,2,4,128]{4,1,3,0,2:T(8,128)(2,1)S(1)} %bitcast.54, bf16[14,256,2,4,128]{4,1,3,0,2:T(8,128)(2,1)} %copy.60, bf16[15,64,4,128]{3,2,1,0:T(4,128)(2,1)S(1)} %reshape.93), kind=kOutput, calls=%fused_computation.15 | convolution fusion | flops 253624320 | bytes 12779520 | tf_op jit(solution)/shard_map/wqhd,wkhd->whqk/dot_general | solution.py:21
  188.7 1.9 copy-done.2
  190.5 1.5 fusion.39
  192.0 11.2 %fusion.21 = bf16[15,64,4,128]{3,1,2,0:T(8,128)(2,1)S(1)} fusion(bf16[14,256,2,4,128]{4,1,3,0,2:T(8,128)(2,1)} %copy.60, bf16[1,256,2,4,128]{4,1,3,0,2:T(8,128)(2,1)S(1)} %bitcast.55, f32[15,4,64]{2,1,0:T(4,128)S(1)} %fusion.39, f32[15,4,64,256]{3,2,1,0:T(8,128)} %copy-done.2), kind=kOutput, calls=%fused_computation.29 | convolution fusion | flops 264933376 | bytes 12794880 | tf_op jit(solution)/shard_map/whqk,wkhd->wqhd/dot_general | solution.py:27
  204.2 1.1 slice.26
  (53 shorter events, 11.8 us)
Async XLA Ops:
  10.8 9.2 %all-to-all-start = ((s32[8,1,4]{2,1,0:T(1,128)}), s32[8,1,4]{2,1,0:T(1,128)S(1)}, u32[]{:S(2)}, u32[]{:S(2)}) async-start(s32[8,1,4]{2,1,0:T(1,128)} %bitcast.2), calls=%async_computation | async-start | bytes 8192 | tf_op jit(solution)/shard_map/all_to_all | solution.py:53
  26.9 45.6 %all-to-all-start.1 = ((bf16[8,4,2,14336]{3,1,2,0:T(4,128)(2,1)}), bf16[8,4,2,14336]{3,1,2,0:T(4,128)(2,1)S(1)}, u32[]{:S(2)}, u32[]{:S(2)}) async-start(bf16[8,4,2,14336]{3,1,2,0:T(4,128)(2,1)} %pad_maximum_fusion.1), calls=%async_computation.1 | async-start | bytes 3670016 | tf_op jit(solution)/shard_map/all_to_all | solution.py:61
  33.7 102.4 %all-gather.2.cloned.1.call-start = ((), (), s32[]{:S(2)}) async-start(), calls=%async_computation.2 | async-start | bytes 8028160 | tf_op jit(solution)/shard_map/all_gather | solution.py:64
  89.7 50.8 %copy-start.4 = (f32[896]{0:T(1024)S(1)}, f32[896]{0:T(1024)}, u32[]{:S(2)}) copy-start(f32[896]{0:T(1024)} %param.10) | copy-start | bytes 10756
  136.1 4.7 %copy-start.1 = (bf16[3584,896]{0,1:T(8,128)(2,1)S(1)}, bf16[3584,896]{0,1:T(8,128)(2,1)}, u32[]{:S(2)}) copy-start(bf16[3584,896]{0,1:T(8,128)(2,1)} %all-gather.2.cloned.1.call-done) | copy-start | bytes 19267588
  140.8 16.2 %copy-start.3 = (bf16[896,512]{1,0:T(8,128)(2,1)S(1)}, bf16[896,512]{1,0:T(8,128)(2,1)}, u32[]{:S(2)}) copy-start(bf16[896,512]{1,0:T(8,128)(2,1)} %param.8) | copy-start | bytes 2752516
  149.5 3.0 %copy-start = (bf16[3584,1024]{0,1:T(8,128)(2,1)}, bf16[3584,1024]{0,1:T(8,128)(2,1)S(1)}, u32[]{:S(2)}) copy-start(bf16[3584,1024]{0,1:T(8,128)(2,1)S(1)} %multiply_convert_fusion) | copy-start | bytes 22020100
  153.5 32.0 %collective-permute-start = (bf16[256,2,4,128]{3,0,2,1:T(8,128)(2,1)}, bf16[256,2,4,128]{3,0,2,1:T(8,128)(2,1)S(1)}, u32[]{:S(2)}, u32[]{:S(2)}) collective-permute-start(bf16[256,2,4,128]{3,0,2,1:T(8,128)(2,1)} %copy.58), channel_id=1, source_target_pairs={{0,4},{4,8},{8,12},{12,16},{16,20},{20,24},{24,28},{1,5},{5,9},{9,... | collective-permute-start | bytes 1572872 | tf_op jit(solution)/shard_map/ppermute | solution.py:17
  188.7 1.9 copy-start.2
Sparse Core Ops, SparseCore 0:
  87.8 48.2 all-gather.1
where the time goes:
time: 215 us; the launch traced here: 212 us
  waiting for transfers between devices  86.5 us (40%)
  local copies, waits for them, and re-layouts  60.2 us (28%)
  matrix products  23 us (11%)
  starting transfers between devices  16.2 us (8%)
  between operations  13.6 us (6%)
  other arithmetic  12.7 us (6%)
    all_gather x1, waiting for transfers between devices, per_device(): lax.all_gather(enc_rows, 'tensor', axis=1, tiled=True).astype(jnp.float32)  46.5 us
    all_to_all x1, waiting for transfers between devices, per_device(): lax.all_to_all(outgoing, 'seq', split_axis=0, concat_axis=0, tiled=True)  38.8 us
    reshape x2, local copies, waits for them, and re-layouts, per_device(): keys_values.reshape(group_count, 4 * group_len, 2, head_count, HEAD_DIM)  27.9 us
    dot_general x1, matrix products, attend(): jnp.einsum('whqk,wkhd->wqhd', weights, kv_win[:, :, 1], preferred_element...  11.2 us
    dot_general x1, matrix products, per_device(): kv_sum = jnp.dot(scaled, projection, preferred_element_type=jnp.float32)  8.67 us
    unnamed x13, local copies, waits for them, and re-layouts  8.17 us
    all_to_all x1, starting transfers between devices, per_device(): lax.all_to_all(outgoing, 'seq', split_axis=0, concat_axis=0, tiled=True)  6.79 us
    all_to_all x1, starting transfers between devices, per_device(): lax.all_to_all(table.reshape(seq_count, slot_cap), 'seq', split_axis=0, c...  6.03 us
  transfers between devices with their start and end apart: 4, of which 3 were waited for; matrix products, arithmetic and copies ran while one was open for 15% of the time, Pallas kernels for 0%

commit v1 on v0

v1 whole, which is shorter than its diff:
```python
import functools
import math

import jax
import jax.numpy as jnp
from jax import lax
from jax.experimental import pallas as pl
from jax.experimental.pallas import tpu as pltpu
from jax.sharding import PartitionSpec as P

HEAD_DIM = 128
LANES = 128
MESH = pl.DeviceIdType.MESH

epsilon = 1e-06


def exchange(seq_count, tensor_count, slot_cap, table_ref, pairs_ref, x_ref, req, req_smem, stage,
             small_sem, ask_send, ask_recv, seq_send, seq_recv, across_send, across_recv,
             mate_send, mate_recv, relay_send, relay_recv):
    me = lax.axis_index("seq")
    ten = lax.axis_index("tensor")
    mate = ten + 1 - 2 * (ten % 2)
    across = (ten + 2) % tensor_count

    def to(k):
        return (me + k) % seq_count

    def source(k):
        return (me + seq_count - k) % seq_count

    barrier = pltpu.get_barrier_semaphore()

    @pl.loop(1, seq_count)
    def _(k):
        pl.semaphore_signal(barrier, inc=1, device_id=(to(k), ten), device_id_type=MESH)

    pl.semaphore_signal(barrier, inc=1, device_id=(me, mate), device_id_type=MESH)
    pl.semaphore_signal(barrier, inc=1, device_id=(me, across), device_id_type=MESH)
    pl.semaphore_wait(barrier, seq_count + 1)

    def ask(k, landing):
        return pltpu.make_async_remote_copy(
            src_ref=table_ref.at[to(k)], dst_ref=req.at[landing],
            send_sem=ask_send.at[k], recv_sem=ask_recv.at[k],
            device_id=(to(k), ten), device_id_type=MESH,
        )

    def move(k, landing):
        return pltpu.make_async_remote_copy(
            src_ref=stage.at[k], dst_ref=x_ref.at[ten, landing],
            send_sem=seq_send.at[k], recv_sem=seq_recv.at[k],
            device_id=(to(k), ten), device_id_type=MESH,
        )

    def share(part, k, send, recv, other):
        block = x_ref.at[part, source(k)]
        return pltpu.make_async_remote_copy(
            src_ref=block, dst_ref=block, send_sem=send.at[k], recv_sem=recv.at[k],
            device_id=(me, other), device_id_type=MESH,
        )

    def to_across(k, part):
        return share(part, k, across_send, across_recv, across)

    def to_mate(k, part):
        return share(part, k, mate_send, mate_recv, mate)

    def relay(k, part):
        return share(part, k, relay_send, relay_recv, mate)

    @pl.loop(1, seq_count)
    def _(k):
        ask(k, me).start()

    req[me] = table_ref[me]

    @pl.loop(1, seq_count)
    def _(k):
        ask(k, source(k)).wait_recv()

    to_scalar = pltpu.make_async_copy(req, req_smem, small_sem.at[0])
    to_scalar.start()
    to_scalar.wait()

    def fill(k):
        for c in range(slot_cap):
            stage[k, c] = pairs_ref[req_smem[to(k), 0, c]]

    @pl.loop(1, seq_count)
    def _(k):
        fill(k)
        move(k, me).start()

    fill(0)
    own = pltpu.make_async_copy(stage.at[0], x_ref.at[ten, me], small_sem.at[1])
    own.start()
    own.wait()
    to_across(0, ten).start()
    to_mate(0, ten).start()

    def pass_on(k):
        to_across(k, across).wait_recv()
        relay(k, across).start()

    @pl.loop(1, seq_count)
    def _(k):
        move(k, source(k)).wait_recv()
        to_across(k, ten).start()
        to_mate(k, ten).start()
        pass_on(k - 1)

    pass_on(seq_count - 1)

    @pl.loop(1, seq_count)
    def _(k):
        ask(k, me).wait_send()
        move(k, me).wait_send()

    @pl.loop(0, seq_count)
    def _(k):
        to_across(k, ten).wait_send()
        to_mate(k, ten).wait_send()
        relay(k, across).wait_send()
        to_mate(k, mate).wait_recv()
        relay(k, (mate + 2) % tensor_count).wait_recv()


def gathered_states(seq_count, tensor_count, slot_cap, table, pairs):
    feats, toks = pairs.shape[1:]
    dma = pltpu.SemaphoreType.DMA
    return pl.pallas_call(
        functools.partial(exchange, seq_count, tensor_count, slot_cap),
        out_shape=jax.ShapeDtypeStruct((tensor_count, seq_count, slot_cap, feats, toks), jnp.bfloat16),
        in_specs=[pl.BlockSpec(memory_space=pltpu.VMEM)] * 2,
        out_specs=pl.BlockSpec(memory_space=pl.ANY),
        scratch_shapes=[
            pltpu.VMEM((seq_count, 1, LANES), jnp.int32),
            pltpu.SMEM((seq_count, 1, LANES), jnp.int32),
            pltpu.VMEM((seq_count, slot_cap, feats, toks), jnp.bfloat16),
            dma((2,)),
        ] + [dma((seq_count,))] * 10,
        compiler_params=pltpu.CompilerParams(
            collective_id=0, has_side_effects=True, vmem_limit_bytes=32 * 1024 * 1024
        ),
    )(table, pairs)


def attend(enc_width, head_count, slots, first_ref, second_ref, weight_ref, gain_ref, query_ref, out_ref):
    def flat(ref):
        return ref[...].reshape(enc_width, -1)

    as_float = jnp.concatenate([flat(first_ref), flat(second_ref)], axis=1).astype(jnp.float32)
    square_sum = jnp.sum(as_float * as_float, axis=0, keepdims=True)
    inv_rms = lax.rsqrt(square_sum / enc_width + epsilon)
    scaled = (as_float * gain_ref[...]).astype(jnp.bfloat16)
    half = head_count * HEAD_DIM
    kv_sum = jnp.dot(weight_ref[...], scaled, preferred_element_type=jnp.float32)
    keys_values = (kv_sum * inv_rms).astype(jnp.bfloat16)
    for h in range(head_count):
        cols = slice(h * HEAD_DIM, (h + 1) * HEAD_DIM)
        keys = keys_values[h * HEAD_DIM : (h + 1) * HEAD_DIM]
        values = keys_values[half + h * HEAD_DIM : half + (h + 1) * HEAD_DIM]
        scores = jnp.dot(query_ref[:, cols], keys, preferred_element_type=jnp.float32) / math.sqrt(HEAD_DIM)
        expo = jnp.exp(scores - jnp.max(scores, axis=-1, keepdims=True))
        weights = (expo / jnp.sum(expo, axis=-1, keepdims=True)).astype(jnp.bfloat16)
        mixed = lax.dot_general(
            weights, values, (((1,), (1,)), ((), ())), preferred_element_type=jnp.float32
        )
        out_ref[:, cols] = mixed.astype(jnp.bfloat16)


def attended_rows(states, slots, weight, gain, query_win, group_len):
    tensor_count, _, feats, toks = states.shape
    rows, cols = query_win.shape
    enc_width = weight.shape[1]
    head_count = cols // HEAD_DIM
    groups = rows // group_len

    def picked(which):
        return pl.BlockSpec(
            (tensor_count, 1, feats, toks), lambda c, slots: (0, slots[2 * c + which], 0, 0)
        )

    return pl.pallas_call(
        functools.partial(attend, enc_width, head_count),
        grid_spec=pltpu.PrefetchScalarGridSpec(
            num_scalar_prefetch=1,
            grid=(groups,),
            in_specs=[
                picked(0),
                picked(1),
                pl.BlockSpec(weight.shape, lambda c, slots: (0, 0)),
                pl.BlockSpec(gain.shape, lambda c, slots: (0, 0)),
                pl.BlockSpec((group_len, cols), lambda c, slots: (c, 0)),
            ],
            out_specs=pl.BlockSpec((group_len, cols), lambda c, slots: (c, 0)),
        ),
        out_shape=jax.ShapeDtypeStruct((rows, cols), jnp.bfloat16),
        compiler_params=pltpu.CompilerParams(vmem_limit_bytes=40 * 1024 * 1024),
    )(slots, states, states, weight, gain, query_win)


def per_device(queries, db_states, enc_gain, kv_weight, shard_ids, offsets):
    seq_count = lax.axis_size("seq")
    tensor_count = lax.axis_size("tensor")
    group_count = shard_ids.shape[0]
    neigh_count = 2 * group_count
    slot_cap = (neigh_count + seq_count - 1) // seq_count
    group_len = db_states.shape[1]
    enc_width = kv_weight.shape[0]
    edge = group_len - 1
    kept = queries.shape[0] - edge

    back = [(i + 1, i) for i in range(seq_count - 1)]
    forth = [(i, i + 1) for i in range(seq_count - 1)]
    next_rows = lax.ppermute(queries[:group_len], "seq", back)

    shard = shard_ids.reshape(neigh_count)
    offset = offsets.reshape(neigh_count)
    place = jnp.arange(neigh_count, dtype=jnp.int32)
    earlier = (shard[:, None] == shard[None, :]) & (place[None, :] < place[:, None])
    rank = jnp.sum(earlier.astype(jnp.int32), axis=1)
    slots = shard * slot_cap + rank
    owner = jnp.arange(seq_count, dtype=jnp.int32)[:, None, None, None]
    lane = jnp.arange(LANES, dtype=jnp.int32)[None, None, :, None]
    named = (shard[None, None, None, :] == owner) & (rank[None, None, None, :] == lane)
    table = jnp.sum(jnp.where(named, offset[None, None, None, :], 0), axis=-1)

    turned = jnp.transpose(db_states, (0, 2, 1))
    pairs = jnp.concatenate([turned[:-1], turned[1:]], axis=2)
    weight = jnp.transpose(kv_weight, (1, 2, 0)).reshape(-1, enc_width)

    states = gathered_states(seq_count, tensor_count, slot_cap, table, pairs)
    states = states.reshape(tensor_count, seq_count * slot_cap, *states.shape[3:])
    query_win = jnp.concatenate([queries[edge:], next_rows[:edge]], axis=0)
    attended = attended_rows(states, slots, weight, enc_gain.reshape(-1, 1), query_win, group_len)
    previous = lax.ppermute(attended[kept - 1 :], "seq", forth)
    return jnp.concatenate([previous[1:], attended[:kept]], axis=0)


def solution(mesh):
    return jax.shard_map(
        per_device,
        mesh=mesh,
        in_specs=(
            P("seq", "tensor"),
            P("seq", None, "tensor"),
            P(),
            P(None, None, "tensor"),
            P("seq", None),
            P("seq", None),
        ),
        out_specs=P("seq", "tensor"),
        check_vma=False,
    )
```

time: 215 us -> 121 us (0.56); the launches traced: 212 us -> 121 us
  Pallas kernels: 0 us -> 96.9 us
  waiting for transfers between devices: 86.5 us -> 4.6 us
  local copies, waits for them, and re-layouts: 60.2 us -> 10 us
  matrix products: 23 us -> 0 us
  between operations: 13.6 us -> 0.14 us
  starting transfers between devices: 16.2 us -> 5.76 us
  other arithmetic: 12.7 us -> 3.56 us
    pallas_call x0 -> x2, Pallas kernels: none -> 96.9 us  [the longest x1 67.9 us: gathered_states(): pl.pallas_call(functools.partial(exchange, seq_count, tensor_count, slot_...]
    all_gather x1 -> x0, waiting for transfers between devices: 46.5 us -> none  [per_device(): lax.all_gather(enc_rows, 'tensor', axis=1, tiled=True).astype(jnp.float32)]
    all_to_all x2 -> x0, waiting for transfers between devices: 40 us -> none  [the longest x1 38.8 us: per_device(): lax.all_to_all(outgoing, 'seq', split_axis=0, concat_axis=0, tiled=True)]
    reshape x5 -> x2, local copies, waits for them, and re-layouts: 30.1 us -> 0.26 us  [the longest x1 0.17 us: per_device(): enc_gain.reshape(-1, 1)]
    dot_general x3 -> x0, matrix products: 23 us -> none  [the longest x1 11.2 us: attend(): jnp.einsum('whqk,wkhd->wqhd', weights, kv_win[:, :, 1], preferred_element...]
    all_to_all x2 -> x0, starting transfers between devices: 12.8 us -> none  [the longest x1 6.79 us: per_device(): lax.all_to_all(outgoing, 'seq', split_axis=0, concat_axis=0, tiled=True)]
    gather x5 -> x0, local copies, waits for them, and re-layouts: 8.18 us -> none  [the longest x1 5.28 us: per_device(): jnp.take(incoming.reshape(seq_count * slot_cap, 2, -1), slot_index, axis=0)]
    unnamed x13 -> x9, local copies, waits for them, and re-layouts: 8.17 us -> 1.29 us
  transfers between devices with their start and end apart: 4 -> 2, of which waited for: 3 -> 1; matrix products, arithmetic and copies ran while one was open for 15% -> 9% of each run, Pallas kernels for 0% -> 56%
where the time goes in v1:
time: 121 us
  Pallas kernels  96.9 us (80%)
  local copies, waits for them, and re-layouts  10 us (8%)
  starting transfers between devices  5.76 us (5%)
  waiting for transfers between devices  4.6 us (4%)
  other arithmetic  3.56 us (3%)
    pallas_call x1, Pallas kernels, gathered_states(): pl.pallas_call(functools.partial(exchange, seq_count, tensor_count, slot_...  67.9 us
    pallas_call x1, Pallas kernels, attended_rows(): pl.pallas_call(functools.partial(attend, enc_width, head_count), grid_spe...  29 us
    transpose x1, local copies, waits for them, and re-layouts, per_device(): weight = jnp.transpose(kv_weight, (1, 2, 0)).reshape(-1, enc_width)  4.65 us
    ppermute x1, waiting for transfers between devices, per_device(): previous = lax.ppermute(attended[kept - 1:], 'seq', forth)  4.6 us
    ppermute x1, starting transfers between devices, per_device(): next_rows = lax.ppermute(queries[:group_len], 'seq', back)  3.27 us
    ppermute x1, starting transfers between devices, per_device(): previous = lax.ppermute(attended[kept - 1:], 'seq', forth)  2.49 us
  transfers between devices with their start and end apart: 2, of which 1 were waited for; matrix products, arithmetic and copies ran while one was open for 9% of the time, Pallas kernels for 56%

profile of v1, /device:TPU:24, one launch (start us, length us, event | category | flops | bytes accessed | tf_op | source)
XLA Modules:
  0.0 121.0 jit_solution(5267954088796694652)
XLA Ops:
  0.0 0.9 slice.27
  0.9 3.3 %collective-permute-start = (bf16[64,512]{1,0:T(8,128)(2,1)S(1)}, bf16[64,512]{1,0:T(8,128)(2,1)S(1)}, u32[]{:S(2)}, u32[]{:S(2)}) collective-permute-start(bf16[64,512]{1,0:T(8,128)(2,1)S(1)} %slice.27), channel_id=1, source_target_pairs={{4,0},{8,4},{12,8},{16,12},{20,16},{24,20},{28,24},{5,1},{9,5},{13... | collective-permute-start | bytes 196616 | tf_op jit(solution)/shard_map/ppermute | solution.py:217
  4.2 0.8 copy.16
  5.0 0.1 reshape.79
  5.1 0.2 convert_reduce_fusion
  5.2 0.1 iota_compare_fusion.1
  5.3 0.1 iota_compare_fusion
  5.4 1.4 %slice.26 = bf16[833,512]{1,0:T(8,128)(2,1)S(1)} slice(bf16[896,512]{1,0:T(8,128)(2,1)} %param.6), slice={[63:896], [0:512]} | slice | bytes 1705984 | tf_op jit(solution)/shard_map/slice | solution.py:236
  6.8 0.1 copy.17
  6.9 0.1 broadcast_in_dim.19
  7.0 0.2 reshape.83.gain_ref
  7.2 0.4 copy.18
  7.6 1.4 %fusion.1 = (bf16[15,224,64]{2,1,0:T(8,128)(2,1)}, bf16[15,224,64]{2,1,0:T(8,128)(2,1)}) fusion(bf16[16,224,64]{2,1,0:T(8,128)(2,1)S(1)} %bitcast.10), kind=kLoop, calls=%fused_computation.10 | loop fusion | bytes 1720320 | tf_op jit(solution)/shard_map/slice | solution.py:231
  9.0 4.7 %copy.19 = bf16[2,512,896]{2,1,0:T(8,128)(2,1)S(1)} copy(bf16[2,512,896]{1,0,2:T(2,128)(2,1)} %bitcast.11) | data formatting | bytes 3670016 | tf_op jit(solution)/shard_map/transpose | solution.py:232
  13.6 1.9 %pad_maximum_fusion.2.pairs_ref = bf16[15,224,128]{2,1,0:T(8,128)(2,1)S(1)} fusion(bf16[15,224,64]{2,1,0:T(8,128)(2,1)} %get-tuple-element.6, bf16[15,224,64]{2,1,0:T(8,128)(2,1)} %get-tuple-element.5), kind=kLoop, calls=%fused_computation.2 | loop fusion | flops 1720320 | bytes 1720320 | tf_op jit(solution)/shard_map/concatenate | solution.py:231
  15.5 0.1 select_reduce_fusion
  15.7 67.9 %shard_map.64 = bf16[4,8,4,224,128]{4,3,2,1,0:T(8,128)(2,1)S(1)} custom-call(s32[8,1,128]{2,1,0:T(1,128)S(1)} %bitcast.9, bf16[15,224,128]{2,1,0:T(8,128)(2,1)S(1)} %pad_maximum_fusion.2.pairs_ref), custom_call_target="tpu_custom_call" | custom-call | tf_op jit(solution)/shard_map/pallas_call | solution.py:132
  83.6 0.0 collective-permute-done
  83.6 0.1 pad_maximum_fusion.query_ref
  83.7 29.0 %shard_map.65 = bf16[896,512]{1,0:T(8,128)(2,1)S(1)} custom-call(s32[28]{0:T(128)S(1)} %multiply_add_fusion.slots, bf16[4,32,224,128]{3,2,1,0:T(8,128)(2,1)S(1)} %bitcast.6, bf16[4,32,224,128]{3,2,1,0:T(8,128)(2,1)S(1)} %bitcast.7, bf16[1024,896]{1,0:T(8,128)(2,1)S(1)} %bitcast.8, f32[896,1]{1,0:T(8,128)S(1)} %reshape.83.gain_ref, ...), custom_call_target="tpu_custom_call" | custom-call | tf_op jit(solution)/shard_map/pallas_call | solution.py:185
  112.6 2.5 %collective-permute-start.1 = (bf16[64,512]{1,0:T(8,128)(2,1)S(1)}, bf16[64,512]{1,0:T(8,128)(2,1)S(1)}, u32[]{:S(2)}, u32[]{:S(2)}) collective-permute-start(bf16[64,512]{1,0:T(8,128)(2,1)S(1)} %slice.35), channel_id=1, source_target_pairs={{0,4},{4,8},{8,12},{12,16},{16,20},{20,24},{24,28},{1,5},{5,9},{9,... | collective-permute-start | bytes 196616 | tf_op jit(solution)/shard_map/ppermute | solution.py:238
  115.1 0.1 slice.37
  115.2 4.6 %collective-permute-done.1 = bf16[64,512]{1,0:T(8,128)(2,1)S(1)} collective-permute-done((bf16[64,512]{1,0:T(8,128)(2,1)S(1)}, bf16[64,512]{1,0:T(8,128)(2,1)S(1)}, u32[]{:S(2)}, u32[]{:S(2)}) %collective-permute-start.1) | collective-permute-done | bytes 65568 | tf_op jit(solution)/shard_map/ppermute | solution.py:238
  119.8 1.1 pad_maximum_fusion.1
  (9 shorter events, 0.0 us)
Async XLA Ops:
  0.0 6.8 %copy-start.2 = (s32[14,2]{0,1:T(2,128)S(1)}, s32[14,2]{0,1:T(2,128)}, u32[]{:S(2)}) copy-start(s32[14,2]{0,1:T(2,128)} %param.11) | copy-start | bytes 340
  0.0 7.0 %copy-start.1 = (f32[896]{0:T(1024)S(1)}, f32[896]{0:T(1024)}, u32[]{:S(2)}) copy-start(f32[896]{0:T(1024)} %param.8) | copy-start | bytes 10756
  0.0 7.1 %copy-start = (bf16[16,64,224]{2,1,0:T(8,128)(2,1)S(1)}, bf16[16,64,224]{2,1,0:T(8,128)(2,1)}, u32[]{:S(2)}) copy-start(bf16[16,64,224]{2,1,0:T(8,128)(2,1)} %param.7) | copy-start | bytes 1376260
  0.9 82.7 %collective-permute-start = (bf16[64,512]{1,0:T(8,128)(2,1)S(1)}, bf16[64,512]{1,0:T(8,128)(2,1)S(1)}, u32[]{:S(2)}, u32[]{:S(2)}) collective-permute-start(bf16[64,512]{1,0:T(8,128)(2,1)S(1)} %slice.27), channel_id=1, source_target_pairs={{4,0},{8,4},{12,8},{16,12},{20,16},{24,20},{28,24},{5,1},{9,5},{13... | collective-permute-start | bytes 196616 | tf_op jit(solution)/shard_map/ppermute | solution.py:217
  112.6 7.2 %collective-permute-start.1 = (bf16[64,512]{1,0:T(8,128)(2,1)S(1)}, bf16[64,512]{1,0:T(8,128)(2,1)S(1)}, u32[]{:S(2)}, u32[]{:S(2)}) collective-permute-start(bf16[64,512]{1,0:T(8,128)(2,1)S(1)} %slice.35), channel_id=1, source_target_pairs={{0,4},{4,8},{8,12},{12,16},{16,20},{20,24},{24,28},{1,5},{5,9},{9,... | collective-permute-start | bytes 196616 | tf_op jit(solution)/shard_map/ppermute | solution.py:238

commit v2 on v1

--- a/solution.py
+++ b/solution.py
@@ -10,13 +10,14 @@
 
 HEAD_DIM = 128
 LANES = 128
+ROWS = 256
 MESH = pl.DeviceIdType.MESH
 
 epsilon = 1e-06
 
 
-def exchange(seq_count, tensor_count, slot_cap, table_ref, pairs_ref, x_ref, req, req_smem, stage,
-             small_sem, ask_send, ask_recv, seq_send, seq_recv, across_send, across_recv,
+def exchange(seq_count, tensor_count, slot_cap, table_ref, pairs_ref, weight_ref, gain_ref, kv_ref,
+             req, req_smem, stage, x_ref, turned, scaled, kv_held, small_sem, out_sem, ask_send, ask_recv, seq_send, seq_recv, across_send, across_recv,
              mate_send, mate_recv, relay_send, relay_recv):
     me = lax.axis_index("seq")
     ten = lax.axis_index("tensor")
@@ -74,6 +75,12 @@
         ask(k, me).start()
 
     req[me] = table_ref[me]
+    enc_width, kv_cols = weight_ref.shape
+
+    @pl.loop(0, kv_cols // LANES)
+    def _(i):
+        cols = pl.ds(pl.multiple_of(i * LANES, LANES), LANES)
+        turned[cols, :] = weight_ref[:, cols].T
 
     @pl.loop(1, seq_count)
     def _(k):
@@ -103,6 +110,34 @@
         to_across(k, across).wait_recv()
         relay(k, across).start()
 
+    def write_out(k):
+        return pltpu.make_async_copy(kv_held.at[k % 2], kv_ref.at[source(k)], out_sem.at[k])
+
+    def project(k):
+        to_mate(k, mate).wait_recv()
+        relay(k, (mate + 2) % tensor_count).wait_recv()
+
+        @pl.when(k >= 2)
+        def _():
+            write_out(k - 2).wait()
+
+        inv_rms = []
+        for c in range(slot_cap):
+            as_float = x_ref[:, source(k), c].reshape(enc_width, LANES).astype(jnp.float32)
+            square_sum = jnp.sum(as_float * as_float, axis=0, keepdims=True)
+            inv_rms.append(lax.rsqrt(square_sum / enc_width + epsilon))
+            scaled[:, c * LANES : (c + 1) * LANES] = (as_float * gain_ref[...]).astype(jnp.bfloat16)
+
+        @pl.loop(0, kv_cols // ROWS)
+        def _(i):
+            rows = pl.ds(pl.multiple_of(i * ROWS, ROWS), ROWS)
+            kv_sum = jnp.dot(turned[rows, :], scaled[...], preferred_element_type=jnp.float32)
+            for c in range(slot_cap):
+                part = kv_sum[:, c * LANES : (c + 1) * LANES] * inv_rms[c]
+                kv_held[k % 2, c, rows, :] = part.astype(jnp.bfloat16)
+
+        write_out(k).start()
+
     @pl.loop(1, seq_count)
     def _(k):
         move(k, source(k)).wait_recv()
@@ -110,7 +145,15 @@
         to_mate(k, ten).start()
         pass_on(k - 1)
 
+        @pl.when(k >= 2)
+        def _():
+            project(k - 2)
+
     pass_on(seq_count - 1)
+
+    @pl.loop(seq_count - 2, seq_count)
+    def _(k):
+        project(k)
 
     @pl.loop(1, seq_count)
     def _(k):
@@ -122,45 +165,44 @@
         to_across(k, ten).wait_send()
         to_mate(k, ten).wait_send()
         relay(k, across).wait_send()
-        to_mate(k, mate).wait_recv()
-        relay(k, (mate + 2) % tensor_count).wait_recv()
-
-
-def gathered_states(seq_count, tensor_count, slot_cap, table, pairs):
+
+    @pl.loop(seq_count - 2, seq_count)
+    def _(k):
+        write_out(k).wait()
+
+
+def gathered_kv(seq_count, tensor_count, slot_cap, table, pairs, weight, gain):
     feats, toks = pairs.shape[1:]
+    enc_width, kv_cols = weight.shape
     dma = pltpu.SemaphoreType.DMA
     return pl.pallas_call(
         functools.partial(exchange, seq_count, tensor_count, slot_cap),
-        out_shape=jax.ShapeDtypeStruct((tensor_count, seq_count, slot_cap, feats, toks), jnp.bfloat16),
-        in_specs=[pl.BlockSpec(memory_space=pltpu.VMEM)] * 2,
+        out_shape=jax.ShapeDtypeStruct((seq_count, slot_cap, kv_cols, toks), jnp.bfloat16),
+        in_specs=[pl.BlockSpec(memory_space=pltpu.VMEM)] * 4,
         out_specs=pl.BlockSpec(memory_space=pl.ANY),
         scratch_shapes=[
             pltpu.VMEM((seq_count, 1, LANES), jnp.int32),
             pltpu.SMEM((seq_count, 1, LANES), jnp.int32),
             pltpu.VMEM((seq_count, slot_cap, feats, toks), jnp.bfloat16),
+            pltpu.VMEM((tensor_count, seq_count, slot_cap, feats, toks), jnp.bfloat16),
+            pltpu.VMEM((kv_cols, enc_width), jnp.bfloat16),
+            pltpu.VMEM((enc_width, slot_cap * toks), jnp.bfloat16),
+            pltpu.VMEM((2, slot_cap, kv_cols, toks), jnp.bfloat16),
             dma((2,)),
-        ] + [dma((seq_count,))] * 10,
+        ] + [dma((seq_count,))] * 11,
         compiler_params=pltpu.CompilerParams(
-            collective_id=0, has_side_effects=True, vmem_limit_bytes=32 * 1024 * 1024
+            collective_id=0, has_side_effects=True, vmem_limit_bytes=54 * 1024 * 1024
         ),
-    )(table, pairs)
-
-
-def attend(enc_width, head_count, slots, first_ref, second_ref, weight_ref, gain_ref, query_ref, out_ref):
-    def flat(ref):
-        return ref[...].reshape(enc_width, -1)
-
-    as_float = jnp.concatenate([flat(first_ref), flat(second_ref)], axis=1).astype(jnp.float32)
-    square_sum = jnp.sum(as_float * as_float, axis=0, keepdims=True)
-    inv_rms = lax.rsqrt(square_sum / enc_width + epsilon)
-    scaled = (as_float * gain_ref[...]).astype(jnp.bfloat16)
+    )(table, pairs, weight, gain)
+
+
+def attend(head_count, slots, first_ref, second_ref, query_ref, out_ref):
     half = head_count * HEAD_DIM
-    kv_sum = jnp.dot(weight_ref[...], scaled, preferred_element_type=jnp.float32)
-    keys_values = (kv_sum * inv_rms).astype(jnp.bfloat16)
     for h in range(head_count):
         cols = slice(h * HEAD_DIM, (h + 1) * HEAD_DIM)
-        keys = keys_values[h * HEAD_DIM : (h + 1) * HEAD_DIM]
-        values = keys_values[half + h * HEAD_DIM : half + (h + 1) * HEAD_DIM]
+        late = slice(half + h * HEAD_DIM, half + (h + 1) * HEAD_DIM)
+        keys = jnp.concatenate([first_ref[0, cols], second_ref[0, cols]], axis=1)
+        values = jnp.concatenate([first_ref[0, late], second_ref[0, late]], axis=1)
         scores = jnp.dot(query_ref[:, cols], keys, preferred_element_type=jnp.float32) / math.sqrt(HEAD_DIM)
         expo = jnp.exp(scores - jnp.max(scores, axis=-1, keepdims=True))
         weights = (expo / jnp.sum(expo, axis=-1, keepdims=True)).astype(jnp.bfloat16)
@@ -170,35 +212,24 @@
         out_ref[:, cols] = mixed.astype(jnp.bfloat16)
 
 
-def attended_rows(states, slots, weight, gain, query_win, group_len):
-    tensor_count, _, feats, toks = states.shape
+def attended_rows(kv, slots, query_win, group_len):
+    _, kv_cols, toks = kv.shape
     rows, cols = query_win.shape
-    enc_width = weight.shape[1]
-    head_count = cols // HEAD_DIM
-    groups = rows // group_len
 
     def picked(which):
-        return pl.BlockSpec(
-            (tensor_count, 1, feats, toks), lambda c, slots: (0, slots[2 * c + which], 0, 0)
-        )
+        return pl.BlockSpec((1, kv_cols, toks), lambda c, slots: (slots[2 * c + which], 0, 0))
 
     return pl.pallas_call(
-        functools.partial(attend, enc_width, head_count),
+        functools.partial(attend, cols // HEAD_DIM),
         grid_spec=pltpu.PrefetchScalarGridSpec(
             num_scalar_prefetch=1,
-            grid=(groups,),
-            in_specs=[
-                picked(0),
-                picked(1),
-                pl.BlockSpec(weight.shape, lambda c, slots: (0, 0)),
-                pl.BlockSpec(gain.shape, lambda c, slots: (0, 0)),
-                pl.BlockSpec((group_len, cols), lambda c, slots: (c, 0)),
-            ],
+            grid=(rows // group_len,),
+            in_specs=[picked(0), picked(1), pl.BlockSpec((group_len, cols), lambda c, slots: (c, 0))],
             out_specs=pl.BlockSpec((group_len, cols), lambda c, slots: (c, 0)),
         ),
         out_shape=jax.ShapeDtypeStruct((rows, cols), jnp.bfloat16),
-        compiler_params=pltpu.CompilerParams(vmem_limit_bytes=40 * 1024 * 1024),
-    )(slots, states, states, weight, gain, query_win)
+        compiler_params=pltpu.CompilerParams(vmem_limit_bytes=32 * 1024 * 1024),
+    )(slots, kv, kv, query_win)
 
 
 def per_device(queries, db_states, enc_gain, kv_weight, shard_ids, offsets):
@@ -229,12 +260,12 @@
 
     turned = jnp.transpose(db_states, (0, 2, 1))
     pairs = jnp.concatenate([turned[:-1], turned[1:]], axis=2)
-    weight = jnp.transpose(kv_weight, (1, 2, 0)).reshape(-1, enc_width)
-
-    states = gathered_states(seq_count, tensor_count, slot_cap, table, pairs)
-    states = states.reshape(tensor_count, seq_count * slot_cap, *states.shape[3:])
+    weight = kv_weight.reshape(enc_width, -1)
+
+    kv = gathered_kv(seq_count, tensor_count, slot_cap, table, pairs, weight, enc_gain.reshape(-1, 1))
+    kv = kv.reshape(seq_count * slot_cap, *kv.shape[2:])
     query_win = jnp.concatenate([queries[edge:], next_rows[:edge]], axis=0)
-    attended = attended_rows(states, slots, weight, enc_gain.reshape(-1, 1), query_win, group_len)
+    attended = attended_rows(kv, slots, query_win, group_len)
     previous = lax.ppermute(attended[kept - 1 :], "seq", forth)
     return jnp.concatenate([previous[1:], attended[:kept]], axis=0)
 

time: 121 us -> 112 us (0.926)
  Pallas kernels: 96.9 us -> 86 us
  local copies, waits for them, and re-layouts: 10 us -> 11.4 us
    pallas_call x2, Pallas kernels: 96.9 us -> 86 us  [the longest x1 74.6 us: gathered_kv(): pl.pallas_call(functools.partial(exchange, seq_count, tensor_count, slot_...]
    unnamed x9 -> x14, local copies, waits for them, and re-layouts: 1.29 us -> 7.72 us
    transpose x1 -> x0, local copies, waits for them, and re-layouts: 4.65 us -> none  [per_device(): weight = jnp.transpose(kv_weight, (1, 2, 0)).reshape(-1, enc_width)]
  transfers between devices with their start and end apart: 2 -> 2, of which waited for: 1 -> 1; matrix products, arithmetic and copies ran while one was open for 9% -> 7% of each run, Pallas kernels for 56% -> 67%
where the time goes in v2:
time: 112 us; the launch traced here: 111 us
  Pallas kernels  86 us (77%)
  local copies, waits for them, and re-layouts  11.4 us (10%)
  starting transfers between devices  5.46 us (5%)
  waiting for transfers between devices  4.81 us (4%)
  other arithmetic  3.63 us (3%)
    pallas_call x1, Pallas kernels, gathered_kv(): pl.pallas_call(functools.partial(exchange, seq_count, tensor_count, slot_...  74.6 us
    pallas_call x1, Pallas kernels, attended_rows(): pl.pallas_call(functools.partial(attend, cols // HEAD_DIM), grid_spec=plt...  11.4 us
    unnamed x14, local copies, waits for them, and re-layouts  7.72 us
    ppermute x1, waiting for transfers between devices, per_device(): previous = lax.ppermute(attended[kept - 1:], 'seq', forth)  4.8 us
    ppermute x1, starting transfers between devices, per_device(): next_rows = lax.ppermute(queries[:group_len], 'seq', back)  3.27 us
  transfers between devices with their start and end apart: 2, of which 1 were waited for; matrix products, arithmetic and copies ran while one was open for 7% of the time, Pallas kernels for 67%

profile of v2, /device:TPU:24, one launch (start us, length us, event | category | flops | bytes accessed | tf_op | source)
XLA Modules:
  0.0 111.4 jit_solution(14774233947668897310)
XLA Ops:
  0.0 0.9 slice.27
  0.9 3.3 %collective-permute-start = (bf16[64,512]{1,0:T(8,128)(2,1)S(1)}, bf16[64,512]{1,0:T(8,128)(2,1)S(1)}, u32[]{:S(2)}, u32[]{:S(2)}) collective-permute-start(bf16[64,512]{1,0:T(8,128)(2,1)S(1)} %slice.27), channel_id=1, source_target_pairs={{4,0},{8,4},{12,8},{16,12},{20,16},{24,20},{28,24},{5,1},{9,5},{13... | collective-permute-start | bytes 196616 | tf_op jit(solution)/shard_map/ppermute | solution.py:248
  4.2 0.8 copy.14
  5.0 0.1 reshape.79
  5.0 0.2 convert_reduce_fusion
  5.2 0.1 iota_compare_fusion
  5.3 0.1 iota_compare_fusion.1
  5.4 1.4 %slice.26 = bf16[833,512]{1,0:T(8,128)(2,1)S(1)} slice(bf16[896,512]{1,0:T(8,128)(2,1)} %param.6), slice={[63:896], [0:512]} | slice | bytes 1705984 | tf_op jit(solution)/shard_map/slice | solution.py:267
  6.8 0.1 copy.15
  6.9 0.1 broadcast_in_dim.19
  7.0 0.4 copy.16
  7.4 0.2 fusion.1
  7.6 1.3 %copy-done.1 = bf16[896,2,512]{2,1,0:T(2,128)(2,1)S(1)} copy-done((bf16[896,2,512]{2,1,0:T(2,128)(2,1)S(1)}, bf16[896,2,512]{2,1,0:T(2,128)(2,1)}, u32[]{:S(2)}) %copy-start.1) | copy-done | bytes 1835032
  8.9 1.8 %copy.18 = bf16[112,8,2,512]{3,1,2,0:T(8,128)(2,1)} copy(bf16[112,8,2,512]{3,2,1,0:T(2,128)(2,1)S(1)} %bitcast.10) | data formatting | bytes 3670016
  10.7 1.0 reshape.83.gain_ref
  11.6 1.4 %pad_maximum_fusion.2.pairs_ref = bf16[15,224,128]{2,1,0:T(8,128)(2,1)} fusion(bf16[15,224,64]{2,1,0:T(8,128)(2,1)S(1)} %get-tuple-element.6, bf16[15,224,64]{2,1,0:T(8,128)(2,1)S(1)} %get-tuple-element.5), kind=kLoop, calls=%fused_computation.2 | loop fusion | flops 1720320 | bytes 1720320 | tf_op jit(solution)/shard_map/concatenate | solution.py:262
  13.0 0.7 select_reduce_fusion
  13.7 74.6 %shard_map.64 = bf16[8,4,1024,128]{3,2,1,0:T(8,128)(2,1)} custom-call(s32[8,1,128]{2,1,0:T(1,128)} %bitcast.12, bf16[15,224,128]{2,1,0:T(8,128)(2,1)} %pad_maximum_fusion.2.pairs_ref, bf16[896,1024]{1,0:T(8,128)(2,1)} %bitcast.9, f32[896,1]{1,0:T(8,128)} %reshape.83.gain_ref), custom_call_target="tpu_custom_call" | custom-call | tf_op jit(solution)/shard_map/pallas_call | solution.py:178
  88.3 0.1 pad_maximum_fusion.query_ref
  88.4 3.4 %copy-done = bf16[8,4,1024,128]{3,2,1,0:T(8,128)(2,1)S(1)} copy-done((bf16[8,4,1024,128]{3,2,1,0:T(8,128)(2,1)S(1)}, bf16[8,4,1024,128]{3,2,1,0:T(8,128)(2,1)}, u32[]{:S(2)}) %copy-start) | copy-done | bytes 8388632
  91.8 11.4 %shard_map.65 = bf16[896,512]{1,0:T(8,128)(2,1)S(1)} custom-call(s32[28]{0:T(128)S(1)} %multiply_add_fusion.slots, bf16[32,1024,128]{2,1,0:T(8,128)(2,1)S(1)} %bitcast.6, bf16[32,1024,128]{2,1,0:T(8,128)(2,1)S(1)} %bitcast.7, bf16[896,512]{1,0:T(8,128)(2,1)S(1)} %pad_maximum_fusion.query_ref), custom_call_target="tpu_custom_call" | custom-call | tf_op jit(solution)/shard_map/pallas_call | solution.py:222
  103.2 2.2 %collective-permute-start.1 = (bf16[64,512]{1,0:T(8,128)(2,1)S(1)}, bf16[64,512]{1,0:T(8,128)(2,1)S(1)}, u32[]{:S(2)}, u32[]{:S(2)}) collective-permute-start(bf16[64,512]{1,0:T(8,128)(2,1)S(1)} %slice.35), channel_id=1, source_target_pairs={{0,4},{4,8},{8,12},{12,16},{16,20},{20,24},{24,28},{1,5},{5,9},{9,... | collective-permute-start | bytes 196616 | tf_op jit(solution)/shard_map/ppermute | solution.py:269
  105.5 4.8 %collective-permute-done.1 = bf16[64,512]{1,0:T(8,128)(2,1)S(1)} collective-permute-done((bf16[64,512]{1,0:T(8,128)(2,1)S(1)}, bf16[64,512]{1,0:T(8,128)(2,1)S(1)}, u32[]{:S(2)}, u32[]{:S(2)}) %collective-permute-start.1) | collective-permute-done | bytes 65568 | tf_op jit(solution)/shard_map/ppermute | solution.py:269
  110.3 1.1 %pad_maximum_fusion.1 = bf16[896,512]{1,0:T(8,128)(2,1)} fusion(bf16[833,512]{1,0:T(8,128)(2,1)S(1)} %slice.37, bf16[63,512]{1,0:T(8,128)(2,1)S(1)} %slice.36), kind=kLoop, calls=%fused_computation.1 | loop fusion | flops 1835008 | bytes 1835008 | tf_op jit(solution)/shard_map/concatenate | solution.py:270
  (13 shorter events, 0.1 us)
Async XLA Ops:
  0.0 6.8 %copy-start.4 = (s32[14,2]{0,1:T(2,128)S(1)}, s32[14,2]{0,1:T(2,128)}, u32[]{:S(2)}) copy-start(s32[14,2]{0,1:T(2,128)} %param.11) | copy-start | bytes 340
  0.0 6.9 %copy-start.2 = (bf16[16,64,224]{2,1,0:T(8,128)(2,1)S(1)}, bf16[16,64,224]{2,1,0:T(8,128)(2,1)}, u32[]{:S(2)}) copy-start(bf16[16,64,224]{2,1,0:T(8,128)(2,1)} %param.7) | copy-start | bytes 1376260
  0.9 87.4 %collective-permute-start = (bf16[64,512]{1,0:T(8,128)(2,1)S(1)}, bf16[64,512]{1,0:T(8,128)(2,1)S(1)}, u32[]{:S(2)}, u32[]{:S(2)}) collective-permute-start(bf16[64,512]{1,0:T(8,128)(2,1)S(1)} %slice.27), channel_id=1, source_target_pairs={{4,0},{8,4},{12,8},{16,12},{20,16},{24,20},{28,24},{5,1},{9,5},{13... | collective-permute-start | bytes 196616 | tf_op jit(solution)/shard_map/ppermute | solution.py:248
  7.4 1.5 %copy-start.1 = (bf16[896,2,512]{2,1,0:T(2,128)(2,1)S(1)}, bf16[896,2,512]{2,1,0:T(2,128)(2,1)}, u32[]{:S(2)}) copy-start(bf16[896,2,512]{2,1,0:T(2,128)(2,1)} %param.9) | copy-start | bytes 5505028
  8.9 1.8 %copy-start.3 = (f32[896]{0:T(1024)S(1)}, f32[896]{0:T(1024)}, u32[]{:S(2)}) copy-start(f32[896]{0:T(1024)} %param.8) | copy-start | bytes 10756
  88.4 3.4 %copy-start = (bf16[8,4,1024,128]{3,2,1,0:T(8,128)(2,1)S(1)}, bf16[8,4,1024,128]{3,2,1,0:T(8,128)(2,1)}, u32[]{:S(2)}) copy-start(bf16[8,4,1024,128]{3,2,1,0:T(8,128)(2,1)} %shard_map.64) | copy-start | bytes 25165828
  103.2 7.1 %collective-permute-start.1 = (bf16[64,512]{1,0:T(8,128)(2,1)S(1)}, bf16[64,512]{1,0:T(8,128)(2,1)S(1)}, u32[]{:S(2)}, u32[]{:S(2)}) collective-permute-start(bf16[64,512]{1,0:T(8,128)(2,1)S(1)} %slice.35), channel_id=1, source_target_pairs={{0,4},{4,8},{8,12},{12,16},{16,20},{20,24},{24,28},{1,5},{5,9},{9,... | collective-permute-start | bytes 196616 | tf_op jit(solution)/shard_map/ppermute | solution.py:269

commit v3 on v2

--- a/solution.py
+++ b/solution.py
@@ -11,6 +11,7 @@
 HEAD_DIM = 128
 LANES = 128
 ROWS = 256
+FLIGHT = 3
 MESH = pl.DeviceIdType.MESH
 
 epsilon = 1e-06
@@ -25,10 +26,15 @@
     across = (ten + 2) % tensor_count
 
     def to(k):
-        return (me + k) % seq_count
-
-    def source(k):
-        return (me + seq_count - k) % seq_count
+        far, near = seq_count // 2 + (k - 1) // 2, k // 2
+        flip = (k % 2) * far + (1 - k % 2) * near
+        bit, other = 1, 0
+        while bit < seq_count:
+            other = other + ((me // bit + flip // bit) % 2) * bit
+            bit *= 2
+        return other
+
+    source = to
 
     barrier = pltpu.get_barrier_semaphore()
 
@@ -75,36 +81,43 @@
         ask(k, me).start()
 
     req[me] = table_ref[me]
-    enc_width, kv_cols = weight_ref.shape
-
-    @pl.loop(0, kv_cols // LANES)
-    def _(i):
-        cols = pl.ds(pl.multiple_of(i * LANES, LANES), LANES)
-        turned[cols, :] = weight_ref[:, cols].T
-
-    @pl.loop(1, seq_count)
-    def _(k):
-        ask(k, source(k)).wait_recv()
-
-    to_scalar = pltpu.make_async_copy(req, req_smem, small_sem.at[0])
-    to_scalar.start()
-    to_scalar.wait()
 
     def fill(k):
         for c in range(slot_cap):
             stage[k, c] = pairs_ref[req_smem[to(k), 0, c]]
 
-    @pl.loop(1, seq_count)
-    def _(k):
-        fill(k)
-        move(k, me).start()
-
+    own_ask = pltpu.make_async_copy(table_ref.at[me], req_smem.at[me], small_sem.at[0])
+    own_ask.start()
+    own_ask.wait()
     fill(0)
     own = pltpu.make_async_copy(stage.at[0], x_ref.at[ten, me], small_sem.at[1])
     own.start()
     own.wait()
     to_across(0, ten).start()
     to_mate(0, ten).start()
+
+    enc_width, kv_cols = weight_ref.shape
+
+    @pl.loop(0, kv_cols // LANES)
+    def _(i):
+        cols = pl.ds(pl.multiple_of(i * LANES, LANES), LANES)
+        turned[cols, :] = weight_ref[:, cols].T
+
+    @pl.loop(1, seq_count)
+    def _(k):
+        ask(k, source(k)).wait_recv()
+
+    to_scalar = pltpu.make_async_copy(req, req_smem, small_sem.at[0])
+    to_scalar.start()
+    to_scalar.wait()
+
+    def send(k):
+        fill(k)
+        move(k, me).start()
+
+    @pl.loop(1, min(FLIGHT + 1, seq_count))
+    def _(k):
+        send(k)
 
     def pass_on(k):
         to_across(k, across).wait_recv()
@@ -140,6 +153,12 @@
 
     @pl.loop(1, seq_count)
     def _(k):
+        move(k, me).wait_send()
+
+        @pl.when(k + FLIGHT < seq_count)
+        def _():
+            send(k + FLIGHT)
+
         move(k, source(k)).wait_recv()
         to_across(k, ten).start()
         to_mate(k, ten).start()
@@ -158,7 +177,6 @@
     @pl.loop(1, seq_count)
     def _(k):
         ask(k, me).wait_send()
-        move(k, me).wait_send()
 
     @pl.loop(0, seq_count)
     def _(k):
@@ -203,9 +221,10 @@
         late = slice(half + h * HEAD_DIM, half + (h + 1) * HEAD_DIM)
         keys = jnp.concatenate([first_ref[0, cols], second_ref[0, cols]], axis=1)
         values = jnp.concatenate([first_ref[0, late], second_ref[0, late]], axis=1)
-        scores = jnp.dot(query_ref[:, cols], keys, preferred_element_type=jnp.float32) / math.sqrt(HEAD_DIM)
-        expo = jnp.exp(scores - jnp.max(scores, axis=-1, keepdims=True))
-        weights = (expo / jnp.sum(expo, axis=-1, keepdims=True)).astype(jnp.bfloat16)
+        scores = jnp.dot(query_ref[:, cols], keys, preferred_element_type=jnp.float32)
+        lowered = scores - jnp.max(scores, axis=-1, keepdims=True)
+        expo = jnp.exp(lowered * (1.0 / math.sqrt(HEAD_DIM)))
+        weights = (expo * (1.0 / jnp.sum(expo, axis=-1, keepdims=True))).astype(jnp.bfloat16)
         mixed = lax.dot_general(
             weights, values, (((1,), (1,)), ((), ())), preferred_element_type=jnp.float32
         )
@@ -228,7 +247,10 @@
             out_specs=pl.BlockSpec((group_len, cols), lambda c, slots: (c, 0)),
         ),
         out_shape=jax.ShapeDtypeStruct((rows, cols), jnp.bfloat16),
-        compiler_params=pltpu.CompilerParams(vmem_limit_bytes=32 * 1024 * 1024),
+        compiler_params=pltpu.CompilerParams(vmem_limit_bytes=60 * 1024 * 1024),
+        cost_estimate=pl.CostEstimate(
+            flops=16 * rows * group_len * cols, bytes_accessed=2 * rows * 16 * cols, transcendentals=0
+        ),
     )(slots, kv, kv, query_win)
 
 
@@ -264,10 +286,11 @@
 
     kv = gathered_kv(seq_count, tensor_count, slot_cap, table, pairs, weight, enc_gain.reshape(-1, 1))
     kv = kv.reshape(seq_count * slot_cap, *kv.shape[2:])
-    query_win = jnp.concatenate([queries[edge:], next_rows[:edge]], axis=0)
-    attended = attended_rows(kv, slots, query_win, group_len)
-    previous = lax.ppermute(attended[kept - 1 :], "seq", forth)
-    return jnp.concatenate([previous[1:], attended[:kept]], axis=0)
+    last_win = jnp.concatenate([queries[kept + edge - 1 :], next_rows[:edge]], axis=0)
+    last = attended_rows(kv, slots[-2:], last_win, group_len)
+    previous = lax.ppermute(last, "seq", forth)
+    rest = attended_rows(kv, slots[:-2], queries[edge : kept + edge - 1], group_len)
+    return jnp.concatenate([previous[1:], rest, last[:1]], axis=0)
 
 
 def solution(mesh):

time: 112 us -> 112 us (level)
  the two profiles are of different devices: /device:TPU:24 before, /device:TPU:0 now
where the time goes in v3:
time: 112 us; the launch traced here: 111 us
  Pallas kernels  89.7 us (80%)
  local copies, waits for them, and re-layouts  11.4 us (10%)
  other arithmetic  5.37 us (5%)
  starting transfers between devices  4.58 us (4%)
    pallas_call x1, Pallas kernels, gathered_kv(): pl.pallas_call(functools.partial(exchange, seq_count, tensor_count, slot_...  72.3 us
    pallas_call x2, Pallas kernels, attended_rows(): pl.pallas_call(functools.partial(attend, cols // HEAD_DIM), grid_spec=plt...  17.5 us
    unnamed x12, local copies, waits for them, and re-layouts  6.07 us
    ppermute x1, starting transfers between devices, per_device(): previous = lax.ppermute(last, 'seq', forth)  3.3 us
    concatenate x1, other arithmetic, per_device(): return jnp.concatenate([previous[1:], rest, last[:1]], axis=0)  2.28 us
  transfers between devices with their start and end apart: 2, of which 0 were waited for; matrix products, arithmetic and copies ran while one was open for 11% of the time, Pallas kernels for 78%

profile of v3, /device:TPU:0, one launch (start us, length us, event | category | flops | bytes accessed | tf_op | source)
XLA Modules:
  0.0 111.2 jit_solution(5243096945422007930)
XLA Ops:
  0.0 0.8 slice.34
  0.8 1.3 %collective-permute-start = (bf16[64,512]{1,0:T(8,128)(2,1)S(1)}, bf16[64,512]{1,0:T(8,128)(2,1)S(1)}, u32[]{:S(2)}, u32[]{:S(2)}) collective-permute-start(bf16[64,512]{1,0:T(8,128)(2,1)S(1)} %slice.34), channel_id=1, source_target_pairs={{4,0},{8,4},{12,8},{16,12},{20,16},{24,20},{28,24},{5,1},{9,5},{13... | collective-permute-start | bytes 196616 | tf_op jit(solution)/shard_map/ppermute | solution.py:270
  2.1 0.8 copy.14
  2.9 0.1 reshape.79
  3.0 0.2 convert_reduce_fusion
  3.3 0.7 slice.33
  4.0 0.8 copy.15
  4.8 0.1 broadcast_in_dim.19
  4.9 1.5 %copy.16 = bf16[16,64,224]{1,2,0:T(8,128)(2,1)S(1)} copy(bf16[16,64,224]{2,1,0:T(8,128)(2,1)} %param.7) | data formatting | bytes 917504 | tf_op args[1]
  6.4 0.2 fusion.1
  6.6 1.3 %copy-done = bf16[896,2,512]{2,1,0:T(2,128)(2,1)S(1)} copy-done((bf16[896,2,512]{2,1,0:T(2,128)(2,1)S(1)}, bf16[896,2,512]{2,1,0:T(2,128)(2,1)}, u32[]{:S(2)}) %copy-start) | copy-done | bytes 1835032
  7.9 1.8 %copy.18 = bf16[112,8,2,512]{3,1,2,0:T(8,128)(2,1)} copy(bf16[112,8,2,512]{3,2,1,0:T(2,128)(2,1)S(1)} %bitcast.13) | data formatting | bytes 3670016
  9.7 1.0 reshape.83.gain_ref
  10.6 0.6 slice.30.slots
  11.2 1.4 %pad_maximum_fusion.1.pairs_ref = bf16[15,224,128]{2,1,0:T(8,128)(2,1)} fusion(bf16[15,224,64]{2,1,0:T(8,128)(2,1)S(1)} %get-tuple-element.6, bf16[15,224,64]{2,1,0:T(8,128)(2,1)S(1)} %get-tuple-element.5), kind=kLoop, calls=%fused_computation.1 | loop fusion | flops 1720320 | bytes 1720320 | tf_op jit(solution)/shard_map/concatenate | solution.py:284
  12.6 0.7 select_reduce_fusion
  13.3 72.3 %shard_map.64 = bf16[8,4,1024,128]{3,2,1,0:T(8,128)(2,1)} custom-call(s32[8,1,128]{2,1,0:T(1,128)} %bitcast.15, bf16[15,224,128]{2,1,0:T(8,128)(2,1)} %pad_maximum_fusion.1.pairs_ref, bf16[896,1024]{1,0:T(8,128)(2,1)} %bitcast.12, f32[896,1]{1,0:T(8,128)} %reshape.83.gain_ref), custom_call_target="tpu_custom_call" | custom-call | tf_op jit(solution)/shard_map/pallas_call | solution.py:196
  85.6 0.7 pad_maximum_fusion.2.query_ref
  86.3 3.2 %shard_map.65 = bf16[64,512]{1,0:T(8,128)(2,1)} custom-call(s32[2]{0:T(128)} %slice.30.slots, bf16[32,1024,128]{2,1,0:T(8,128)(2,1)} %bitcast.7, bf16[32,1024,128]{2,1,0:T(8,128)(2,1)} %bitcast.8, bf16[64,512]{1,0:T(8,128)(2,1)} %pad_maximum_fusion.2.query_ref), custom_call_target="tpu_custom_call" | custom-call | flops 33554432 | bytes 1048576 | tf_op jit(solution)/shard_map/pallas_call | solution.py:241
  89.5 3.3 %collective-permute-start.1 = (bf16[64,512]{1,0:T(8,128)(2,1)}, bf16[64,512]{1,0:T(8,128)(2,1)S(1)}, u32[]{:S(2)}, u32[]{:S(2)}) collective-permute-start(bf16[64,512]{1,0:T(8,128)(2,1)} %shard_map.65), channel_id=1, source_target_pairs={{0,4},{4,8},{8,12},{12,16},{16,20},{20,24},{24,28},{1,5},{5,9},{9,... | collective-permute-start | bytes 196616 | tf_op jit(solution)/shard_map/ppermute | solution.py:291
  92.8 1.1 slice.38.query_ref
  93.9 14.2 %shard_map.66 = bf16[832,512]{1,0:T(8,128)(2,1)} custom-call(s32[26]{0:T(128)} %bitcast.16, bf16[32,1024,128]{2,1,0:T(8,128)(2,1)} %bitcast.9, bf16[32,1024,128]{2,1,0:T(8,128)(2,1)} %bitcast.10, bf16[832,512]{1,0:T(8,128)(2,1)} %slice.38.query_ref), custom_call_target="tpu_custom_call" | custom-call | flops 436207616 | bytes 13631488 | tf_op jit(solution)/shard_map/pallas_call | solution.py:241
  108.2 0.7 slice.44
  108.9 2.3 %pad_maximum_fusion = bf16[896,512]{1,0:T(8,128)(2,1)} fusion(bf16[1,512]{1,0:T(2,128)(2,1)S(1)} %slice.44, bf16[832,512]{1,0:T(8,128)(2,1)} %shard_map.66, bf16[63,512]{1,0:T(8,128)(2,1)S(1)} %slice.43), kind=kLoop, calls=%fused_computation | loop fusion | flops 2752512 | bytes 1835008 | tf_op jit(solution)/shard_map/concatenate | solution.py:293
  (13 shorter events, 0.2 us)
Async XLA Ops:
  0.8 84.8 %collective-permute-start = (bf16[64,512]{1,0:T(8,128)(2,1)S(1)}, bf16[64,512]{1,0:T(8,128)(2,1)S(1)}, u32[]{:S(2)}, u32[]{:S(2)}) collective-permute-start(bf16[64,512]{1,0:T(8,128)(2,1)S(1)} %slice.34), channel_id=1, source_target_pairs={{4,0},{8,4},{12,8},{16,12},{20,16},{24,20},{28,24},{5,1},{9,5},{13... | collective-permute-start | bytes 196616 | tf_op jit(solution)/shard_map/ppermute | solution.py:270
  3.3 7.3 %copy-start.3 = (s32[28]{0:T(128)}, s32[28]{0:T(128)S(1)}, u32[]{:S(2)}) copy-start(s32[28]{0:T(128)S(1)} %multiply_add_fusion) | copy-start | bytes 340
  6.4 1.5 %copy-start = (bf16[896,2,512]{2,1,0:T(2,128)(2,1)S(1)}, bf16[896,2,512]{2,1,0:T(2,128)(2,1)}, u32[]{:S(2)}) copy-start(bf16[896,2,512]{2,1,0:T(2,128)(2,1)} %param.9) | copy-start | bytes 5505028
  7.9 1.8 %copy-start.2 = (f32[896]{0:T(1024)S(1)}, f32[896]{0:T(1024)}, u32[]{:S(2)}) copy-start(f32[896]{0:T(1024)} %param.8) | copy-start | bytes 10756
  86.3 6.5 %copy-start.1 = (bf16[896,512]{1,0:T(8,128)(2,1)S(1)}, bf16[896,512]{1,0:T(8,128)(2,1)}, u32[]{:S(2)}) copy-start(bf16[896,512]{1,0:T(8,128)(2,1)} %param.6) | copy-start | bytes 2752516
  89.5 19.4 %collective-permute-start.1 = (bf16[64,512]{1,0:T(8,128)(2,1)}, bf16[64,512]{1,0:T(8,128)(2,1)S(1)}, u32[]{:S(2)}, u32[]{:S(2)}) collective-permute-start(bf16[64,512]{1,0:T(8,128)(2,1)} %shard_map.65), channel_id=1, source_target_pairs={{0,4},{4,8},{8,12},{12,16},{16,20},{20,24},{24,28},{1,5},{5,9},{9,... | collective-permute-start | bytes 196616 | tf_op jit(solution)/shard_map/ppermute | solution.py:291

commit v4 on v2

--- a/solution.py
+++ b/solution.py
@@ -196,40 +196,48 @@
     )(table, pairs, weight, gain)
 
 
-def attend(head_count, slots, first_ref, second_ref, query_ref, out_ref):
+def attend(head_count, group_len, slots, *refs):
+    *kv_refs, query_ref, out_ref = refs
     half = head_count * HEAD_DIM
-    for h in range(head_count):
-        cols = slice(h * HEAD_DIM, (h + 1) * HEAD_DIM)
-        late = slice(half + h * HEAD_DIM, half + (h + 1) * HEAD_DIM)
-        keys = jnp.concatenate([first_ref[0, cols], second_ref[0, cols]], axis=1)
-        values = jnp.concatenate([first_ref[0, late], second_ref[0, late]], axis=1)
-        scores = jnp.dot(query_ref[:, cols], keys, preferred_element_type=jnp.float32) / math.sqrt(HEAD_DIM)
-        expo = jnp.exp(scores - jnp.max(scores, axis=-1, keepdims=True))
-        weights = (expo / jnp.sum(expo, axis=-1, keepdims=True)).astype(jnp.bfloat16)
-        mixed = lax.dot_general(
-            weights, values, (((1,), (1,)), ((), ())), preferred_element_type=jnp.float32
-        )
-        out_ref[:, cols] = mixed.astype(jnp.bfloat16)
+    for g in range(len(kv_refs) // 2):
+        pair = kv_refs[2 * g : 2 * g + 2]
+        rows = slice(g * group_len, (g + 1) * group_len)
+        for h in range(head_count):
+            cols = slice(h * HEAD_DIM, (h + 1) * HEAD_DIM)
+            late = slice(half + h * HEAD_DIM, half + (h + 1) * HEAD_DIM)
+            keys = jnp.concatenate([ref[0, cols] for ref in pair], axis=1)
+            values = jnp.concatenate([ref[0, late] for ref in pair], axis=1)
+            scores = jnp.dot(query_ref[rows, cols], keys, preferred_element_type=jnp.float32)
+            lowered = scores - jnp.max(scores, axis=-1, keepdims=True)
+            expo = jnp.exp(lowered * (1.0 / math.sqrt(HEAD_DIM)))
+            weights = (expo * (1.0 / jnp.sum(expo, axis=-1, keepdims=True))).astype(jnp.bfloat16)
+            mixed = lax.dot_general(
+                weights, values, (((1,), (1,)), ((), ())), preferred_element_type=jnp.float32
+            )
+            out_ref[rows, cols] = mixed.astype(jnp.bfloat16)
 
 
 def attended_rows(kv, slots, query_win, group_len):
     _, kv_cols, toks = kv.shape
     rows, cols = query_win.shape
+    at_once = 2 if (rows // group_len) % 2 == 0 else 1
+    picks = 2 * at_once
 
     def picked(which):
-        return pl.BlockSpec((1, kv_cols, toks), lambda c, slots: (slots[2 * c + which], 0, 0))
-
+        return pl.BlockSpec((1, kv_cols, toks), lambda c, slots: (slots[picks * c + which], 0, 0))
+
+    tile = pl.BlockSpec((at_once * group_len, cols), lambda c, slots: (c, 0))
     return pl.pallas_call(
-        functools.partial(attend, cols // HEAD_DIM),
+        functools.partial(attend, cols // HEAD_DIM, group_len),
         grid_spec=pltpu.PrefetchScalarGridSpec(
             num_scalar_prefetch=1,
-            grid=(rows // group_len,),
-            in_specs=[picked(0), picked(1), pl.BlockSpec((group_len, cols), lambda c, slots: (c, 0))],
-            out_specs=pl.BlockSpec((group_len, cols), lambda c, slots: (c, 0)),
+            grid=(rows // (at_once * group_len),),
+            in_specs=[picked(i) for i in range(picks)] + [tile],
+            out_specs=tile,
         ),
         out_shape=jax.ShapeDtypeStruct((rows, cols), jnp.bfloat16),
-        compiler_params=pltpu.CompilerParams(vmem_limit_bytes=32 * 1024 * 1024),
-    )(slots, kv, kv, query_win)
+        compiler_params=pltpu.CompilerParams(vmem_limit_bytes=60 * 1024 * 1024),
+    )(slots, *[kv] * picks, query_win)
 
 
 def per_device(queries, db_states, enc_gain, kv_weight, shard_ids, offsets):

time: 112 us -> 112 us (level)
  local copies, waits for them, and re-layouts: 11.4 us -> 8.92 us
  other arithmetic: 3.63 us -> 5.14 us
  Pallas kernels: 86 us -> 87.4 us
    unnamed x14 -> x12, local copies, waits for them, and re-layouts: 7.72 us -> 4.35 us
    pallas_call x1, Pallas kernels: 11.4 us -> 12.8 us  [attended_rows(): pl.pallas_call(functools.partial(attend, cols // HEAD_DIM, group_len), gr...]
  transfers between devices with their start and end apart: 2 -> 2, of which waited for: 1 -> 1; matrix products, arithmetic and copies ran while one was open for 7% -> 8% of each run, Pallas kernels for 67% -> 67%
where the time goes in v4:
time: 112 us
  Pallas kernels  87.4 us (78%)
  local copies, waits for them, and re-layouts  8.92 us (8%)
  starting transfers between devices  5.43 us (5%)
  other arithmetic  5.14 us (5%)
  waiting for transfers between devices  4.89 us (4%)
    pallas_call x1, Pallas kernels, gathered_kv(): pl.pallas_call(functools.partial(exchange, seq_count, tensor_count, slot_...  74.6 us
    pallas_call x1, Pallas kernels, attended_rows(): pl.pallas_call(functools.partial(attend, cols // HEAD_DIM, group_len), gr...  12.8 us
    ppermute x1, waiting for transfers between devices, per_device(): previous = lax.ppermute(attended[kept - 1:], 'seq', forth)  4.89 us
    unnamed x12, local copies, waits for them, and re-layouts  4.35 us
    ppermute x1, starting transfers between devices, per_device(): next_rows = lax.ppermute(queries[:group_len], 'seq', back)  3.27 us
  transfers between devices with their start and end apart: 2, of which 1 were waited for; matrix products, arithmetic and copies ran while one was open for 8% of the time, Pallas kernels for 67%

profile of v4, /device:TPU:24, one launch (start us, length us, event | category | flops | bytes accessed | tf_op | source)
XLA Modules:
  0.0 111.8 jit_solution(7598471819987891165)
XLA Ops:
  0.0 0.9 slice.27
  0.9 3.3 %collective-permute-start = (bf16[64,512]{1,0:T(8,128)(2,1)S(1)}, bf16[64,512]{1,0:T(8,128)(2,1)S(1)}, u32[]{:S(2)}, u32[]{:S(2)}) collective-permute-start(bf16[64,512]{1,0:T(8,128)(2,1)S(1)} %slice.27), channel_id=1, source_target_pairs={{4,0},{8,4},{12,8},{16,12},{20,16},{24,20},{28,24},{5,1},{9,5},{13... | collective-permute-start | bytes 196616 | tf_op jit(solution)/shard_map/ppermute | solution.py:256
  4.2 0.8 copy.14
  5.0 0.1 reshape.79
  5.0 0.2 convert_reduce_fusion
  5.2 0.6 multiply_add_fusion.slots
  5.8 0.1 iota_compare_fusion
  6.0 1.4 %slice.26 = bf16[833,512]{1,0:T(8,128)(2,1)S(1)} slice(bf16[896,512]{1,0:T(8,128)(2,1)} %param.6), slice={[63:896], [0:512]} | slice | bytes 1705984 | tf_op jit(solution)/shard_map/slice | solution.py:275
  7.3 0.1 copy.15
  7.4 0.1 broadcast_in_dim.19
  7.5 0.4 copy.16
  8.0 0.2 fusion.1
  8.2 1.3 %copy-done = bf16[896,2,512]{2,1,0:T(2,128)(2,1)S(1)} copy-done((bf16[896,2,512]{2,1,0:T(2,128)(2,1)S(1)}, bf16[896,2,512]{2,1,0:T(2,128)(2,1)}, u32[]{:S(2)}) %copy-start) | copy-done | bytes 1835032
  9.5 1.8 %copy.18 = bf16[112,8,2,512]{3,1,2,0:T(8,128)(2,1)} copy(bf16[112,8,2,512]{3,2,1,0:T(2,128)(2,1)S(1)} %bitcast.12) | data formatting | bytes 3670016
  11.3 1.0 reshape.83.gain_ref
  12.2 1.4 %pad_maximum_fusion.2.pairs_ref = bf16[15,224,128]{2,1,0:T(8,128)(2,1)} fusion(bf16[15,224,64]{2,1,0:T(8,128)(2,1)S(1)} %get-tuple-element.6, bf16[15,224,64]{2,1,0:T(8,128)(2,1)S(1)} %get-tuple-element.5), kind=kLoop, calls=%fused_computation.2 | loop fusion | flops 1720320 | bytes 1720320 | tf_op jit(solution)/shard_map/concatenate | solution.py:270
  13.6 0.7 select_reduce_fusion
  14.3 74.6 %shard_map.64 = bf16[8,4,1024,128]{3,2,1,0:T(8,128)(2,1)} custom-call(s32[8,1,128]{2,1,0:T(1,128)} %bitcast.14, bf16[15,224,128]{2,1,0:T(8,128)(2,1)} %pad_maximum_fusion.2.pairs_ref, bf16[896,1024]{1,0:T(8,128)(2,1)} %bitcast.11, f32[896,1]{1,0:T(8,128)} %reshape.83.gain_ref), custom_call_target="tpu_custom_call" | custom-call | tf_op jit(solution)/shard_map/pallas_call | solution.py:178
  88.9 1.0 pad_maximum_fusion.refs_4_
  89.9 12.8 %shard_map.65 = bf16[896,512]{1,0:T(8,128)(2,1)} custom-call(s32[28]{0:T(128)} %multiply_add_fusion.slots, bf16[32,1024,128]{2,1,0:T(8,128)(2,1)} %bitcast.6, bf16[32,1024,128]{2,1,0:T(8,128)(2,1)} %bitcast.7, bf16[32,1024,128]{2,1,0:T(8,128)(2,1)} %bitcast.8, bf16[32,1024,128]{2,1,0:T(8,128)(2,1)} %bitcast.9, bf16[896,512]{1,0:T(8,128)(2,1)} %pad_maximum_fusion.refs_4_), custom_call_target="tpu_custom_call" | custom-call | tf_op jit(solution)/shard_map/pallas_call | solution.py:230
  102.7 0.9 slice.35
  103.6 2.2 %collective-permute-start.1 = (bf16[64,512]{1,0:T(8,128)(2,1)S(1)}, bf16[64,512]{1,0:T(8,128)(2,1)S(1)}, u32[]{:S(2)}, u32[]{:S(2)}) collective-permute-start(bf16[64,512]{1,0:T(8,128)(2,1)S(1)} %slice.35), channel_id=1, source_target_pairs={{0,4},{4,8},{8,12},{12,16},{16,20},{20,24},{24,28},{1,5},{5,9},{9,... | collective-permute-start | bytes 196616 | tf_op jit(solution)/shard_map/ppermute | solution.py:277
  105.8 4.9 %collective-permute-done.1 = bf16[64,512]{1,0:T(8,128)(2,1)S(1)} collective-permute-done((bf16[64,512]{1,0:T(8,128)(2,1)S(1)}, bf16[64,512]{1,0:T(8,128)(2,1)S(1)}, u32[]{:S(2)}, u32[]{:S(2)}) %collective-permute-start.1) | collective-permute-done | bytes 65568 | tf_op jit(solution)/shard_map/ppermute | solution.py:277
  110.7 1.1 %pad_maximum_fusion.1 = bf16[896,512]{1,0:T(8,128)(2,1)} fusion(bf16[833,512]{1,0:T(8,128)(2,1)S(1)} %slice-done, bf16[63,512]{1,0:T(8,128)(2,1)S(1)} %slice.36), kind=kLoop, calls=%fused_computation.1 | loop fusion | flops 1835008 | bytes 1835008 | tf_op jit(solution)/shard_map/concatenate | solution.py:278
  (12 shorter events, 0.1 us)
Async XLA Ops:
  0.0 7.3 %copy-start.3 = (s32[14,2]{0,1:T(2,128)S(1)}, s32[14,2]{0,1:T(2,128)}, u32[]{:S(2)}) copy-start(s32[14,2]{0,1:T(2,128)} %param.11) | copy-start | bytes 340
  0.0 7.5 %copy-start.1 = (bf16[16,64,224]{2,1,0:T(8,128)(2,1)S(1)}, bf16[16,64,224]{2,1,0:T(8,128)(2,1)}, u32[]{:S(2)}) copy-start(bf16[16,64,224]{2,1,0:T(8,128)(2,1)} %param.7) | copy-start | bytes 1376260
  0.9 88.0 %collective-permute-start = (bf16[64,512]{1,0:T(8,128)(2,1)S(1)}, bf16[64,512]{1,0:T(8,128)(2,1)S(1)}, u32[]{:S(2)}, u32[]{:S(2)}) collective-permute-start(bf16[64,512]{1,0:T(8,128)(2,1)S(1)} %slice.27), channel_id=1, source_target_pairs={{4,0},{8,4},{12,8},{16,12},{20,16},{24,20},{28,24},{5,1},{9,5},{13... | collective-permute-start | bytes 196616 | tf_op jit(solution)/shard_map/ppermute | solution.py:256
  7.9 1.5 %copy-start = (bf16[896,2,512]{2,1,0:T(2,128)(2,1)S(1)}, bf16[896,2,512]{2,1,0:T(2,128)(2,1)}, u32[]{:S(2)}) copy-start(bf16[896,2,512]{2,1,0:T(2,128)(2,1)} %param.9) | copy-start | bytes 5505028
  9.5 1.8 %copy-start.2 = (f32[896]{0:T(1024)S(1)}, f32[896]{0:T(1024)}, u32[]{:S(2)}) copy-start(f32[896]{0:T(1024)} %param.8) | copy-start | bytes 10756
  102.7 8.0 %slice-start = ((bf16[896,512]{1,0:T(8,128)(2,1)}), bf16[833,512]{1,0:T(8,128)(2,1)S(1)}, s32[]{:S(2)}) async-start(bf16[896,512]{1,0:T(8,128)(2,1)} %shard_map.65), calls=%async_computation | async-start | bytes 1720320 | tf_op jit(solution)/shard_map/slice | solution.py:278
  103.6 7.0 %collective-permute-start.1 = (bf16[64,512]{1,0:T(8,128)(2,1)S(1)}, bf16[64,512]{1,0:T(8,128)(2,1)S(1)}, u32[]{:S(2)}, u32[]{:S(2)}) collective-permute-start(bf16[64,512]{1,0:T(8,128)(2,1)S(1)} %slice.35), channel_id=1, source_target_pairs={{0,4},{4,8},{8,12},{12,16},{16,20},{20,24},{24,28},{1,5},{5,9},{9,... | collective-permute-start | bytes 196616 | tf_op jit(solution)/shard_map/ppermute | solution.py:277

commit v5 on v4

--- a/solution.py
+++ b/solution.py
@@ -175,6 +175,8 @@
     feats, toks = pairs.shape[1:]
     enc_width, kv_cols = weight.shape
     dma = pltpu.SemaphoreType.DMA
+    states = 2 * (tensor_count + 1) * seq_count * slot_cap * feats * toks
+    need = states + 6 * enc_width * kv_cols + 4 * slot_cap * kv_cols * toks
     return pl.pallas_call(
         functools.partial(exchange, seq_count, tensor_count, slot_cap),
         out_shape=jax.ShapeDtypeStruct((seq_count, slot_cap, kv_cols, toks), jnp.bfloat16),
@@ -191,7 +193,7 @@
             dma((2,)),
         ] + [dma((seq_count,))] * 11,
         compiler_params=pltpu.CompilerParams(
-            collective_id=0, has_side_effects=True, vmem_limit_bytes=54 * 1024 * 1024
+            collective_id=0, has_side_effects=True, vmem_limit_bytes=need + 10 * 1024 * 1024
         ),
     )(table, pairs, weight, gain)
 
@@ -236,7 +238,7 @@
             out_specs=tile,
         ),
         out_shape=jax.ShapeDtypeStruct((rows, cols), jnp.bfloat16),
-        compiler_params=pltpu.CompilerParams(vmem_limit_bytes=60 * 1024 * 1024),
+        compiler_params=pltpu.CompilerParams(vmem_limit_bytes=24 * 1024 * 1024),
     )(slots, *[kv] * picks, query_win)
 
 

time: 112 us -> 101 us (0.902)
  Pallas kernels: 87.4 us -> 82.5 us
  other arithmetic: 5.14 us -> 2.13 us
  local copies, waits for them, and re-layouts: 8.92 us -> 6.14 us
    pallas_call x1, Pallas kernels: 74.6 us -> 72.1 us  [gathered_kv(): pl.pallas_call(functools.partial(exchange, seq_count, tensor_count, slot_...]
    pallas_call x1, Pallas kernels: 12.8 us -> 10.4 us  [attended_rows(): pl.pallas_call(functools.partial(attend, cols // HEAD_DIM, group_len), gr...]
  transfers between devices with their start and end apart: 2 -> 2, of which waited for: 1 -> 1; matrix products, arithmetic and copies ran while one was open for 8% -> 5% of each run, Pallas kernels for 67% -> 71%
where the time goes in v5:
time: 101 us
  Pallas kernels  82.5 us (82%)
  local copies, waits for them, and re-layouts  6.14 us (6%)
  starting transfers between devices  5.47 us (5%)
  waiting for transfers between devices  4.79 us (5%)
  other arithmetic  2.13 us (2%)
    pallas_call x1, Pallas kernels, gathered_kv(): pl.pallas_call(functools.partial(exchange, seq_count, tensor_count, slot_...  72.1 us
    pallas_call x1, Pallas kernels, attended_rows(): pl.pallas_call(functools.partial(attend, cols // HEAD_DIM, group_len), gr...  10.4 us
    ppermute x1, waiting for transfers between devices, per_device(): previous = lax.ppermute(attended[kept - 1:], 'seq', forth)  4.79 us
    ppermute x1, starting transfers between devices, per_device(): next_rows = lax.ppermute(queries[:group_len], 'seq', back)  3.27 us
    unnamed x12, local copies, waits for them, and re-layouts  3.24 us
    ppermute x1, starting transfers between devices, per_device(): previous = lax.ppermute(attended[kept - 1:], 'seq', forth)  2.2 us
  transfers between devices with their start and end apart: 2, of which 1 were waited for; matrix products, arithmetic and copies ran while one was open for 5% of the time, Pallas kernels for 71%

profile of v5, /device:TPU:24, one launch (start us, length us, event | category | flops | bytes accessed | tf_op | source)
XLA Modules:
  0.0 101.2 jit_solution(7659614542023045634)
XLA Ops:
  0.0 0.9 slice.27
  0.9 3.3 %collective-permute-start = (bf16[64,512]{1,0:T(8,128)(2,1)S(1)}, bf16[64,512]{1,0:T(8,128)(2,1)S(1)}, u32[]{:S(2)}, u32[]{:S(2)}) collective-permute-start(bf16[64,512]{1,0:T(8,128)(2,1)S(1)} %slice.27), channel_id=1, source_target_pairs={{4,0},{8,4},{12,8},{16,12},{20,16},{24,20},{28,24},{5,1},{9,5},{13... | collective-permute-start | bytes 196616 | tf_op jit(solution)/shard_map/ppermute | solution.py:258
  4.2 0.8 copy.14
  5.0 0.1 reshape.79
  5.0 0.2 convert_reduce_fusion
  5.2 0.1 iota_compare_fusion
  5.3 0.1 iota_compare_fusion.1
  5.4 1.4 %slice.26 = bf16[833,512]{1,0:T(8,128)(2,1)S(1)} slice(bf16[896,512]{1,0:T(8,128)(2,1)} %param.6), slice={[63:896], [0:512]} | slice | bytes 1705984 | tf_op jit(solution)/shard_map/slice | solution.py:277
  6.8 0.1 copy.15
  6.9 0.1 broadcast_in_dim.19
  7.0 0.4 copy.16
  7.4 0.2 fusion.1
  7.6 1.3 %copy-done = bf16[896,2,512]{2,1,0:T(2,128)(2,1)S(1)} copy-done((bf16[896,2,512]{2,1,0:T(2,128)(2,1)S(1)}, bf16[896,2,512]{2,1,0:T(2,128)(2,1)}, u32[]{:S(2)}) %copy-start) | copy-done | bytes 1835032
  8.9 0.5 copy.18
  9.4 0.2 copy-done.2
  9.6 0.2 reshape.83.gain_ref
  9.7 0.5 pad_maximum_fusion.2.pairs_ref
  10.2 0.1 select_reduce_fusion
  10.4 72.1 %shard_map.64 = bf16[8,4,1024,128]{3,2,1,0:T(8,128)(2,1)S(1)} custom-call(s32[8,1,128]{2,1,0:T(1,128)S(1)} %bitcast.11, bf16[15,224,128]{2,1,0:T(8,128)(2,1)S(1)} %pad_maximum_fusion.2.pairs_ref, bf16[896,1024]{1,0:T(8,128)(2,1)S(1)} %bitcast.10, f32[896,1]{1,0:T(8,128)S(1)} %reshape.83.gain_ref), custom_call_target="tpu_custom_call" | custom-call | tf_op jit(solution)/shard_map/pallas_call | solution.py:180
  82.5 0.1 pad_maximum_fusion.refs_4_
  82.6 10.4 %shard_map.65 = bf16[896,512]{1,0:T(8,128)(2,1)S(1)} custom-call(s32[28]{0:T(128)S(1)} %multiply_add_fusion.slots, bf16[32,1024,128]{2,1,0:T(8,128)(2,1)S(1)} %bitcast.6, bf16[32,1024,128]{2,1,0:T(8,128)(2,1)S(1)} %bitcast.7, bf16[32,1024,128]{2,1,0:T(8,128)(2,1)S(1)} %bitcast.8, bf16[32,1024,128]{2,1,0:T(8,128)(2,1)S(1)} %bitcast.9, ...), custom_call_target="tpu_custom_call" | custom-call | tf_op jit(solution)/shard_map/pallas_call | solution.py:232
  93.0 2.2 %collective-permute-start.1 = (bf16[64,512]{1,0:T(8,128)(2,1)S(1)}, bf16[64,512]{1,0:T(8,128)(2,1)S(1)}, u32[]{:S(2)}, u32[]{:S(2)}) collective-permute-start(bf16[64,512]{1,0:T(8,128)(2,1)S(1)} %slice.35), channel_id=1, source_target_pairs={{0,4},{4,8},{8,12},{12,16},{16,20},{20,24},{24,28},{1,5},{5,9},{9,... | collective-permute-start | bytes 196616 | tf_op jit(solution)/shard_map/ppermute | solution.py:279
  95.3 4.8 %collective-permute-done.1 = bf16[64,512]{1,0:T(8,128)(2,1)S(1)} collective-permute-done((bf16[64,512]{1,0:T(8,128)(2,1)S(1)}, bf16[64,512]{1,0:T(8,128)(2,1)S(1)}, u32[]{:S(2)}, u32[]{:S(2)}) %collective-permute-start.1) | collective-permute-done | bytes 65568 | tf_op jit(solution)/shard_map/ppermute | solution.py:279
  100.1 1.1 %pad_maximum_fusion.1 = bf16[896,512]{1,0:T(8,128)(2,1)} fusion(bf16[833,512]{1,0:T(8,128)(2,1)S(1)} %slice.37, bf16[63,512]{1,0:T(8,128)(2,1)S(1)} %slice.36), kind=kLoop, calls=%fused_computation.1 | loop fusion | flops 1835008 | bytes 1835008 | tf_op jit(solution)/shard_map/concatenate | solution.py:280
  (11 shorter events, 0.1 us)
Async XLA Ops:
  0.0 6.8 %copy-start.3 = (s32[14,2]{0,1:T(2,128)S(1)}, s32[14,2]{0,1:T(2,128)}, u32[]{:S(2)}) copy-start(s32[14,2]{0,1:T(2,128)} %param.11) | copy-start | bytes 340
  0.0 6.9 %copy-start.1 = (bf16[16,64,224]{2,1,0:T(8,128)(2,1)S(1)}, bf16[16,64,224]{2,1,0:T(8,128)(2,1)}, u32[]{:S(2)}) copy-start(bf16[16,64,224]{2,1,0:T(8,128)(2,1)} %param.7) | copy-start | bytes 1376260
  0.9 81.6 %collective-permute-start = (bf16[64,512]{1,0:T(8,128)(2,1)S(1)}, bf16[64,512]{1,0:T(8,128)(2,1)S(1)}, u32[]{:S(2)}, u32[]{:S(2)}) collective-permute-start(bf16[64,512]{1,0:T(8,128)(2,1)S(1)} %slice.27), channel_id=1, source_target_pairs={{4,0},{8,4},{12,8},{16,12},{20,16},{24,20},{28,24},{5,1},{9,5},{13... | collective-permute-start | bytes 196616 | tf_op jit(solution)/shard_map/ppermute | solution.py:258
  7.4 1.5 %copy-start = (bf16[896,2,512]{2,1,0:T(2,128)(2,1)S(1)}, bf16[896,2,512]{2,1,0:T(2,128)(2,1)}, u32[]{:S(2)}) copy-start(bf16[896,2,512]{2,1,0:T(2,128)(2,1)} %param.9) | copy-start | bytes 5505028
  8.9 0.7 copy-start.2
  93.0 7.1 %collective-permute-start.1 = (bf16[64,512]{1,0:T(8,128)(2,1)S(1)}, bf16[64,512]{1,0:T(8,128)(2,1)S(1)}, u32[]{:S(2)}, u32[]{:S(2)}) collective-permute-start(bf16[64,512]{1,0:T(8,128)(2,1)S(1)} %slice.35), channel_id=1, source_target_pairs={{0,4},{4,8},{8,12},{12,16},{16,20},{20,24},{24,28},{1,5},{5,9},{9,... | collective-permute-start | bytes 196616 | tf_op jit(solution)/shard_map/ppermute | solution.py:279
